TPU v7x, 32 devices: a whole 2x2x4 slice. The times are simulated.
32 devices in a mesh: seq: 16 (over z, y, x), batch: 2 (over core).
Axes of the slice: x: 2, y: 2, z: 4, core: 2. Of those that a mesh axis runs over, the one named last changes fastest.
Arguments:
- layer_input_tokens: bfloat16 [16, 4096, 768], P('batch', 'seq'), may hold values from -6 to 6
- cotangent: bfloat16 [16, 4096, 768], P('batch', 'seq'), may hold values from -6 to 6
- weight_in: float32 [768, 3072], P(None, ('seq', 'batch')), may hold values from -0.21875 to 0.21875
- weight_out: float32 [3072, 768], P(('seq', 'batch')), may hold values from -0.109375 to 0.109375
- bias_ff: float32 [3072], P(('seq', 'batch')), may hold values from -1.5 to 1.5
- norm_vec: float32 [5, 768], P(None, ('seq', 'batch')), may hold values from -1.75 to 1.75, as said below
- moment_in: float32 [768, 3072], P(None, ('seq', 'batch')), may hold values from -2 to 2
- average_in: float32 [768, 3072], P(None, ('seq', 'batch')), may hold values from -0.21875 to 0.21875
- moment_out: float32 [3072, 768], P(('seq', 'batch')), may hold values from -4 to 4
- average_out: float32 [3072, 768], P(('seq', 'batch')), may hold values from -0.109375 to 0.109375
- moment_bias: float32 [3072], P(('seq', 'batch')), may hold values from -2 to 2
- average_bias: float32 [3072], P(('seq', 'batch')), may hold values from -1.5 to 1.5
- moment_norm: float32 [5, 768], P(None, ('seq', 'batch')), may hold values from -6 to 6
- average_norm: float32 [5, 768], P(None, ('seq', 'batch')), may hold values from 0.1 to 1.9
Outputs:
- layer_out: float32 [16, 4096, 768], P('batch', 'seq')
- tokens_grad: float32 [16, 4096, 768], P('batch', 'seq')
- moment_in_new: float32 [768, 3072], P(None, ('seq', 'batch'))
- weight_in_new: float32 [768, 3072], P(None, ('seq', 'batch'))
- average_in_new: float32 [768, 3072], P(None, ('seq', 'batch'))
- moment_out_new: float32 [3072, 768], P(('seq', 'batch'))
- weight_out_new: float32 [3072, 768], P(('seq', 'batch'))
- average_out_new: float32 [3072, 768], P(('seq', 'batch'))
- moment_bias_new: float32 [3072], P(('seq', 'batch'))
- bias_ff_new: float32 [3072], P(('seq', 'batch'))
- average_bias_new: float32 [3072], P(('seq', 'batch'))
- moment_norm_new: float32 [5, 768], P(None, ('seq', 'batch'))
- norm_vec_new: float32 [5, 768], P(None, ('seq', 'batch'))
- average_norm_new: float32 [5, 768], P(None, ('seq', 'batch'))
Inputs may be any that keep to these rules, and one draw needn't show every extreme that they name: `norm_vec`: rows 0 and 2 are gains between 0.25 and 1.75; rows 1, 3 and 4 are biases.
All inputs are finite; a program needn't handle non-finite values.
Results may differ from a plain program's by a relative error of at most 0.0055.
Values may be sent and summed in bfloat16 or wider, within the bound.
A program may use at most 320 MiB of HBM per device.

v0:
```python
import math

import jax
import jax.numpy as jnp
from jax import lax
from jax.sharding import PartitionSpec as P

EPSILON = 1e-05
MOMENTUM = 0.9
AVG_DECAY = 0.9
RATE_MATRIX = 0.02
RATE_VECTOR = 0.1


def trig_angles(width):
    index = jnp.arange(width, dtype=jnp.int32)
    angle = (index[:, None] * index[None, :] % width).astype(jnp.float32) * (2.0 * math.pi / width)
    scale = 1.0 / math.sqrt(width)
    return (jnp.cos(angle) * scale, jnp.sin(angle) * scale)


def hidden_table(width, sequence_portions):
    cosine, sine = trig_angles(width)
    slice_width = width // sequence_portions
    cosine = cosine.reshape(width, sequence_portions, 1, slice_width)
    sine = sine.reshape(width, sequence_portions, 1, slice_width)
    return jnp.concatenate([cosine, sine], axis=2).reshape(width, 2 * width).astype(jnp.bfloat16)


def sequence_table(length):
    cosine, sine = trig_angles(length)
    return jnp.stack([cosine, -sine], axis=1).astype(jnp.bfloat16)


def norm_forward(value, gain, bias):
    center = value - jnp.mean(value, axis=-1, keepdims=True)
    spread = jnp.mean(center * center, axis=-1, keepdims=True)
    inverse = lax.rsqrt(spread + EPSILON)
    normed = center * inverse
    return (normed * gain + bias, normed, inverse)


def norm_backward(grad, normed, inverse, gain):
    scaled = grad * gain
    return inverse * (
        scaled
        - jnp.mean(scaled, axis=-1, keepdims=True)
        - normed * jnp.mean(scaled * normed, axis=-1, keepdims=True)
    )


def gelu_exact(value):
    return jax.nn.gelu(value, approximate=False)


def nesterov(weight, moment, average, grad, rate, scale):
    scaled = grad * scale
    moment_new = MOMENTUM * moment + scaled
    weight_new = weight - rate * (scaled + MOMENTUM * moment_new)
    average_new = AVG_DECAY * average + (1.0 - AVG_DECAY) * weight_new
    return (moment_new, weight_new, average_new)


def on_device(
    layer_input_tokens,
    cotangent,
    weight_in,
    weight_out,
    bias_ff,
    norm_vec,
    moment_in,
    average_in,
    moment_out,
    average_out,
    moment_bias,
    average_bias,
    moment_norm,
    average_norm,
):
    sequence_total, local_len, width = layer_input_tokens.shape
    seq_parts = lax.axis_size("seq")
    length = local_len * seq_parts
    slice_width = width // seq_parts
    rows = sequence_total * local_len
    hidden_trig_lookup = hidden_table(width, seq_parts)
    seq_tab = sequence_table(length)
    first_low, second_low = (
        lax.all_gather(weight_in.astype(jnp.bfloat16), ("seq", "batch"), axis=1, tiled=True),
        lax.all_gather(weight_out.astype(jnp.bfloat16), ("seq", "batch"), axis=0, tiled=True),
    )
    bias_full, vectors = (
        lax.all_gather(bias_ff, ("seq", "batch"), axis=0, tiled=True),
        lax.all_gather(norm_vec, ("seq", "batch"), axis=1, tiled=True),
    )
    both = jnp.einsum(
        "gmn,nr->grm", layer_input_tokens, hidden_trig_lookup, preferred_element_type=jnp.float32
    ).astype(jnp.bfloat16)
    piece = lax.all_to_all(both, "seq", split_axis=1, concat_axis=2, tiled=True)
    count = piece.shape[0]
    split = piece.reshape(count, 2, slice_width, length)
    mixed_slices = jnp.einsum(
        "lck,scdk->sdl", seq_tab, split, preferred_element_type=jnp.float32
    ).astype(jnp.bfloat16)
    mixed_cols = lax.all_to_all(mixed_slices, "seq", split_axis=2, concat_axis=1, tiled=True)
    mixed = jnp.swapaxes(mixed_cols, 1, 2)
    tokens_f = layer_input_tokens.astype(jnp.float32).reshape(rows, width)
    hidden, normed_one, inverse_one = norm_forward(
        tokens_f + mixed.astype(jnp.float32).reshape(rows, width), vectors[0], vectors[1]
    )
    hidden_low = hidden.astype(jnp.bfloat16)
    pre = jnp.dot(hidden_low, first_low, preferred_element_type=jnp.float32) + bias_full
    act = gelu_exact(pre).astype(jnp.bfloat16)
    ffo = jnp.dot(act, second_low, preferred_element_type=jnp.float32) + vectors[4]
    result, normed_two, inverse_two = norm_forward(hidden + ffo, vectors[2], vectors[3])
    first_back, second_back = (
        lax.all_gather(weight_in.astype(jnp.bfloat16), ("seq", "batch"), axis=1, tiled=True),
        lax.all_gather(weight_out.astype(jnp.bfloat16), ("seq", "batch"), axis=0, tiled=True),
    )
    grad_out = cotangent.astype(jnp.float32).reshape(rows, width)
    dgain_two = jnp.sum(grad_out * normed_two, axis=0)
    dbias_two = jnp.sum(grad_out, axis=0)
    dresid_two = norm_backward(grad_out, normed_two, inverse_two, vectors[2])
    dffo = dresid_two.astype(jnp.bfloat16)
    dbias_out = jnp.sum(dffo.astype(jnp.float32), axis=0)
    dweight_out = jnp.einsum("tf,td->fd", act, dffo, preferred_element_type=jnp.float32)
    dact = jnp.einsum("td,fd->tf", dffo, second_back, preferred_element_type=jnp.float32)
    gelu_pull = jax.vjp(gelu_exact, pre)[1]
    dpre = gelu_pull(dact)[0].astype(jnp.bfloat16)
    dbias_ff = jnp.sum(dpre.astype(jnp.float32), axis=0)
    dweight_in = jnp.einsum("td,tf->df", hidden_low, dpre, preferred_element_type=jnp.float32)
    dhidden = dresid_two + jnp.einsum(
        "tf,df->td", dpre, first_back, preferred_element_type=jnp.float32
    )
    dgain_one = jnp.sum(dhidden * normed_one, axis=0)
    dbias_one = jnp.sum(dhidden, axis=0)
    dresid_one = norm_backward(dhidden, normed_one, inverse_one, vectors[0])
    dmix = jnp.swapaxes(
        dresid_one.astype(jnp.bfloat16).reshape(sequence_total, local_len, width), 1, 2
    )
    piece = lax.all_to_all(dmix, "seq", split_axis=1, concat_axis=2, tiled=True)
    count = piece.shape[0]
    back = jnp.einsum("lck,sdl->scdk", seq_tab, piece, preferred_element_type=jnp.float32)
    dboth_slices = back.reshape(count, 2 * slice_width, length).astype(jnp.bfloat16)
    gradient_both_halves = lax.all_to_all(
        dboth_slices, "seq", split_axis=2, concat_axis=1, tiled=True
    )
    tokens_grad = dresid_one + jnp.einsum(
        "frc,vr->fcv", gradient_both_halves, hidden_trig_lookup, preferred_element_type=jnp.float32
    ).reshape(rows, width)
    gradient_vectors = jnp.stack([dgain_one, dbias_one, dgain_two, dbias_two, dbias_out], axis=0)
    grad_in, grad_out_w, grad_bias, grad_norm = (
        lax.psum_scatter(dweight_in, ("seq", "batch"), scatter_dimension=1, tiled=True),
        lax.psum_scatter(dweight_out, ("seq", "batch"), scatter_dimension=0, tiled=True),
        lax.psum_scatter(dbias_ff, ("seq", "batch"), scatter_dimension=0, tiled=True),
        lax.psum_scatter(gradient_vectors, ("seq", "batch"), scatter_dimension=1, tiled=True),
    )
    total_tokens = sequence_total * lax.axis_size("batch") * length
    scale = total_tokens ** (-0.5)
    m_in, w_in_new, a_in = nesterov(weight_in, moment_in, average_in, grad_in, RATE_MATRIX, scale)
    m_out, w_out_new, a_out = nesterov(
        weight_out, moment_out, average_out, grad_out_w, RATE_MATRIX, scale
    )
    m_bias, b_new, a_bias = nesterov(
        bias_ff, moment_bias, average_bias, grad_bias, RATE_VECTOR, scale
    )
    m_norm, n_new, a_norm = nesterov(
        norm_vec, moment_norm, average_norm, grad_norm, RATE_VECTOR, scale
    )
    layer_out = result.reshape(sequence_total, local_len, width)
    tokens_grad = tokens_grad.reshape(sequence_total, local_len, width)
    return (
        layer_out,
        tokens_grad,
        m_in,
        w_in_new,
        a_in,
        m_out,
        w_out_new,
        a_out,
        m_bias,
        b_new,
        a_bias,
        m_norm,
        n_new,
        a_norm,
    )


def solution(mesh):
    return jax.shard_map(
        on_device,
        mesh=mesh,
        in_specs=(
            P("batch", "seq", None),
            P("batch", "seq", None),
            P(None, ("seq", "batch")),
            P(("seq", "batch"), None),
            P(("seq", "batch")),
            P(None, ("seq", "batch")),
            P(None, ("seq", "batch")),
            P(None, ("seq", "batch")),
            P(("seq", "batch"), None),
            P(("seq", "batch"), None),
            P(("seq", "batch")),
            P(("seq", "batch")),
            P(None, ("seq", "batch")),
            P(None, ("seq", "batch")),
        ),
        out_specs=(
            P("batch", "seq", None),
            P("batch", "seq", None),
            P(None, ("seq", "batch")),
            P(None, ("seq", "batch")),
            P(None, ("seq", "batch")),
            P(("seq", "batch"), None),
            P(("seq", "batch"), None),
            P(("seq", "batch"), None),
            P(("seq", "batch")),
            P(("seq", "batch")),
            P(("seq", "batch")),
            P(None, ("seq", "batch")),
            P(None, ("seq", "batch")),
            P(None, ("seq", "batch")),
        ),
        check_vma=False,
    )
```

profile of v0, /device:TPU:24, one launch (start us, length us, event | category | flops | bytes accessed | tf_op | source)
XLA Modules:
  0.0 1222.2 jit_solution(11483778238561888400)
XLA Ops:
  7.2 10.5 cosine_multiply_fusion
  18.0 5.4 convert_bitcast_fusion
  23.4 17.1 %copy.77 = bf16[8,1536,256]{2,0,1:T(8,128)(2,1)} copy(bf16[8,1536,256]{2,1,0:T(8,128)(2,1)S(1)} %convert_bitcast_fusion) | data formatting | bytes 12582912 | tf_op jit(solution)/shard_map/convert_element_type | solution.py:97
  40.5 7.1 all-to-all-start
  48.6 270.6 %negate_convert_fusion = (bf16[4096,1,4096]{2,0,1:T(8,128)(2,1)}, bf16[4096,1,4096]{2,0,1:T(8,128)(2,1)}) fusion(), kind=kLoop, calls=%fused_computation.7 | loop fusion | flops 318767104 | bytes 67108864 | tf_op jit(solution)/shard_map/convert.5
  319.2 9.1 copy.103
  328.3 10.4 reshape.279
  338.7 32.9 %bitcast_convert_fusion = bf16[8,48,4096]{2,1,0:T(8,128)(2,1)S(1)} fusion(bf16[8,2,48,4096]{3,2,1,0:T(8,128)(2,1)} %reshape.279, bf16[4096,1,4096]{2,0,1:T(8,128)(2,1)} %get-tuple-element.62, bf16[4096,1,4096]{2,0,1:T(8,128)(2,1)} %get-tuple-element.63), kind=kOutput, calls=%fused_computation.48 | convolution fusion | flops 25804931072 | bytes 76546048 | tf_op jit(solution)/shard_map/lck,scdk->sdl/dot_general | solution.py:101
  371.6 7.7 copy.79
  379.3 16.9 %reshape.302 = bf16[16,2,49152]{2,1,0:T(2,128)(2,1)} reshape(bf16[4096,8,48]{2,1,0:T(8,128)(2,1)} %bitcast.122) | data formatting | bytes 6291456
  396.3 7.2 all-to-all-start.1
  408.9 105.7 %all-gather = f32[32,24,5]{1,2,0:T(8,128)S(1)} all-gather(f32[1,24,5]{1,2,0:T(8,128)S(1)} %bitcast.144), channel_id=1, replica_groups=mesh['seq'=16,'batch'=2] {'seq','batch'}, dimensions={0}, use_global_device_ids=true | all-gather | bytes 15840 | tf_op jit(solution)/shard_map/all_gather | solution.py:93
  518.2 41.1 %all-reduce = f32[3072]{0:T(1024)S(1)} all-reduce(f32[3072]{0:T(1024)S(1)} %dynamic-update-slice), channel_id=1, replica_groups=mesh['seq'=16,'batch'=2] {'seq','batch'}, use_global_device_ids=true, to_apply=%add | all-reduce | flops 3072 | bytes 24576
  559.4 14.4 %reshape.303 = bf16[4096,8,48]{2,1,0:T(8,128)(2,1)} reshape(bf16[16,2,49152]{2,1,0:T(2,128)(2,1)} %all-to-all-done.1) | data formatting | bytes 6291456
  573.8 8.3 copy.80
  591.3 6.6 copy.82
  606.3 64.9 %multiply_convert_fusion.1 = (bf16[2048,3072]{1,0:T(8,128)(2,1)}, f32[2048,3072]{1,0:T(8,128)}, f32[2048,3072]{1,0:T(8,128)}) fusion(f32[3072]{0:T(1024)S(1)} %all-reduce, bf16[2048,768]{1,0:T(8,128)(2,1)S(1)} %get-tuple-element.50, bf16[768,3072]{0,1:T(8,128)(2,1)} %all-gather.4.cloned.1.call-done), kind=kOutput, calls=%fused_computation.18 | convolution fusion | flops 10078912512 | bytes 70791168 | tf_op jit(solution)/shard_map/dot_general | solution.py:111
  671.2 15.8 %fusion.40 = (f32[2048]{0:T(1024)S(1)}, f32[2048,768]{1,0:T(8,128)S(1)}) fusion(f32[768]{0:T(1024)S(1)} %copy-done.36, bf16[2048,3072]{1,0:T(8,128)(2,1)} %get-tuple-element.45, bf16[3072,768]{1,0:T(8,128)(2,1)} %all-gather.6.cloned.1.call-done, f32[768]{0:T(1024)S(1)} %copy-done.32, f32[2048,768]{1,0:T(8,128)} %get-tuple-element.51, f32[768]{0:T(1024)S(1)} %copy-done.24), kind=kOutput, calls=%fused_computation.112 | convolution fusion | flops 9671538688 | bytes 29901824 | tf_op jit(solution)/shard_map/dot_general | solution.py:113
  699.6 15.6 %fusion.32 = f32[3072,768]{1,0:T(8,128)} fusion(bf16[2048,3072]{1,0:T(8,128)(2,1)} %get-tuple-element.45, f32[2048,768]{1,0:T(8,128)S(1)} %get-tuple-element.36), kind=kOutput, calls=%fused_computation.106 | convolution fusion | flops 9665249280 | bytes 28311552 | tf_op jit(solution)/shard_map/tf,td->fd/dot_general | solution.py:125
  715.2 32.9 %convert_reduce_fusion = (f32[3072]{0:T(1024)S(1)}, bf16[2048,3072]{1,0:T(8,128)(2,1)}) fusion(f32[2048,3072]{1,0:T(8,128)} %get-tuple-element.46, bf16[3072,768]{1,0:T(8,128)(2,1)} %all-gather.6.cloned.1.call-done, f32[2048,768]{1,0:T(8,128)} %copy-done.4, f32[2048,3072]{1,0:T(8,128)} %get-tuple-element.56, f32[3072]{0:T(1024)S(1)} %all-reduce), kind=kOutput, calls=%fused_computation.16 | convolution fusion | flops 9772200960 | bytes 73949184 | tf_op jit(solution)/shard_map/td,fd->tf/dot_general | solution.py:126
  748.2 19.7 %multiply_reduce_fusion = (f32[768]{0:T(1024)S(1)}, f32[2048]{0:T(1024)S(1)}, f32[2048]{0:T(1024)S(1)}, f32[768]{0:T(1024)S(1)}, f32[2048,768]{1,0:T(8,128)S(1)}) fusion(f32[8,256,768]{2,1,0:T(8,128)} %copy.82, f32[2048]{0:T(1024)S(1)} %bitcast.140, f32[2048]{0:T(1024)S(1)} %bitcast.137, f32[768]{0:T(1024)S(1)} %copy-done.24, f32[2048,768]{1,0:T(8,128)} %copy-done.4, ...), kind=kOutput, calls=%fused_computation.51 | convolution fusion | flops 9679398912 | bytes 36217856 | tf_op jit(solution)/shard_map/tf,df->td/dot_general | solution.py:131
  767.9 8.1 fusion.37
  779.5 7.1 all-to-all-start.2
  786.6 16.7 %fusion.41 = f32[768,3072]{0,1:T(8,128)} fusion(bf16[2048,768]{1,0:T(8,128)(2,1)} %copy-done.6, bf16[2048,3072]{1,0:T(8,128)(2,1)} %get-tuple-element.61), kind=kOutput, calls=%fused_computation.113 | convolution fusion | flops 9663676416 | bytes 25165824 | tf_op jit(solution)/shard_map/td,tf->df/dot_general | solution.py:130
  803.3 68.9 %all-to-all-done.2 = bf16[8,768,256]{2,0,1:T(8,128)(2,1)S(1)} async-done(((bf16[8,768,256]{2,0,1:T(8,128)(2,1)}), bf16[8,768,256]{2,0,1:T(8,128)(2,1)S(1)}, u32[]{:S(2)}, u32[]{:S(2)}) %all-to-all-start.2) | async-done | bytes 3145760 | tf_op jit(solution)/shard_map/all_to_all | solution.py:140
  879.9 34.3 %fusion.14 = bf16[8,48,2,4096]{3,1,2,0:T(8,128)(2,1)} fusion(bf16[4096,1,4096]{2,0,1:T(8,128)(2,1)} %get-tuple-element.62, bf16[4096,1,4096]{2,0,1:T(8,128)(2,1)} %get-tuple-element.63, bf16[8,48,4096,1]{2,1,0,3:T(8,128)(2,1)S(1)} %reshape.293), kind=kOutput, calls=%fused_computation.32 | convolution fusion | flops 25907167232 | bytes 76546048 | tf_op jit(solution)/shard_map/lck,sdl->scdk/dot_general | solution.py:142
  914.3 11.7 copy.87
  926.1 13.0 %all-to-all-start.3 = ((bf16[8,96,4096]{1,0,2:T(8,128)(2,1)}), bf16[8,96,4096]{1,0,2:T(8,128)(2,1)}, u32[]{:S(2)}, u32[]{:S(2)}) async-start(bf16[8,96,4096]{1,0,2:T(8,128)(2,1)} %copy.87), calls=%async_computation.3 | async-start | bytes 16777216 | tf_op jit(solution)/shard_map/all_to_all | solution.py:144
  939.2 239.6 %all-reduce.3 = (f32[3072]{0:T(1024)S(1)}, f32[5,768]{1,0:T(8,128)S(1)}) all-reduce(f32[3072]{0:T(1024)S(1)} %get-tuple-element.60, f32[5,768]{1,0:T(8,128)S(1)} %stack.30), channel_id=4, replica_groups=mesh['seq'=16,'batch'=2] {'seq','batch'}, use_global_device_ids=true, to_apply=%region_11.12.clone | all-reduce | flops 6912 | bytes 55296
  1184.1 11.8 copy.89
  1195.9 8.8 copy.90
  1204.7 10.7 convolution_add_fusion.1
  (141 shorter events, 56.8 us)
Async XLA Ops:
  40.5 278.7 %all-to-all-start = ((bf16[8,1536,256]{2,0,1:T(8,128)(2,1)}), bf16[8,1536,256]{2,0,1:T(8,128)(2,1)}, u32[]{:S(2)}, u32[]{:S(2)}) async-start(bf16[8,1536,256]{2,0,1:T(8,128)(2,1)} %copy.77), calls=%async_computation | async-start | bytes 12582912 | tf_op jit(solution)/shard_map/all_to_all | solution.py:98
  47.6 558.6 %all-gather.4.cloned.1.call-start = ((), (), s32[]{:S(2)}) async-start(), calls=%async_computation.6 | async-start | bytes 4866048 | tf_op jit(solution)/shard_map/all_gather | solution.py:88
  379.3 24.2 %copy-start.9 = (f32[96,768]{1,0:T(8,128)S(1)}, f32[96,768]{1,0:T(8,128)}, u32[]{:S(2)}) copy-start(f32[96,768]{1,0:T(8,128)} %param.17) | copy-start | bytes 884740
  396.3 119.1 %copy-start.1 = (bf16[8,256,768]{2,1,0:T(8,128)(2,1)S(1)}, bf16[8,256,768]{2,1,0:T(8,128)(2,1)}, u32[]{:S(2)}) copy-start(bf16[8,256,768]{2,1,0:T(8,128)(2,1)} %param.15) | copy-start | bytes 9437188
  396.3 163.1 %all-to-all-start.1 = ((bf16[16,2,49152]{2,1,0:T(2,128)(2,1)}), bf16[16,2,49152]{2,1,0:T(2,128)(2,1)}, u32[]{:S(2)}, u32[]{:S(2)}) async-start(bf16[16,2,49152]{2,1,0:T(2,128)(2,1)} %reshape.302), calls=%async_computation.1 | async-start | bytes 6291456 | tf_op jit(solution)/shard_map/all_to_all | solution.py:104
  403.4 114.6 %copy-start.37 = (f32[96]{0:T(128)S(1)}, f32[96]{0:T(128)}, u32[]{:S(2)}) copy-start(f32[96]{0:T(128)} %param.18) | copy-start | bytes 1156
  403.4 267.7 %all-gather.6.cloned.1.call-start = ((), (), s32[]{:S(2)}) async-start(), calls=%async_computation.7 | async-start | bytes 4866048 | tf_op jit(solution)/shard_map/all_gather | solution.py:89
  404.2 776.0 %reduce-scatter.6.cloned.1.call-start = ((), (), s32[]{:S(2)}) async-start(), calls=%async_computation.9 | async-start | bytes 9732096 | tf_op jit(solution)/shard_map/reduce_scatter | solution.py:153
  515.4 86.1 %copy-start.23 = (f32[768]{0:T(1024)}, f32[768]{0:T(1024)S(1)}, u32[]{:S(2)}) copy-start(f32[768]{0:T(1024)S(1)} %get-tuple-element.26) | copy-start | bytes 9220
  515.4 86.2 %copy-start.31 = (f32[768]{0:T(1024)}, f32[768]{0:T(1024)S(1)}, u32[]{:S(2)}) copy-start(f32[768]{0:T(1024)S(1)} %get-tuple-element.25) | copy-start | bytes 9220
  606.2 64.9 %copy-start.6 = (bf16[2048,768]{1,0:T(8,128)(2,1)}, bf16[2048,768]{1,0:T(8,128)(2,1)S(1)}, u32[]{:S(2)}) copy-start(bf16[2048,768]{1,0:T(8,128)(2,1)S(1)} %get-tuple-element.50) | copy-start | bytes 9437188
  606.2 64.9 %copy-start.24 = (f32[768]{0:T(1024)S(1)}, f32[768]{0:T(1024)}, u32[]{:S(2)}) copy-start(f32[768]{0:T(1024)} %copy-done.23) | copy-start | bytes 9220
  606.2 64.9 %copy-start.32 = (f32[768]{0:T(1024)S(1)}, f32[768]{0:T(1024)}, u32[]{:S(2)}) copy-start(f32[768]{0:T(1024)} %copy-done.31) | copy-start | bytes 9220
  606.2 64.9 %copy-start.36 = (f32[768]{0:T(1024)S(1)}, f32[768]{0:T(1024)}, u32[]{:S(2)}) copy-start(f32[768]{0:T(1024)} %get-tuple-element.24) | copy-start | bytes 9220
  715.2 33.0 %copy-start.18 = (f32[1,2,8,128]{3,1,2,0:T(2,128)S(1)}, f32[1,2,8,128]{3,1,2,0:T(2,128)}, u32[]{:S(2)}) copy-start(f32[1,2,8,128]{3,1,2,0:T(2,128)} %copy-done.17) | copy-start | bytes 24580
  715.2 32.9 %copy-start.20 = (f32[1,2,8,128]{3,1,2,0:T(2,128)S(1)}, f32[1,2,8,128]{3,1,2,0:T(2,128)}, u32[]{:S(2)}) copy-start(f32[1,2,8,128]{3,1,2,0:T(2,128)} %copy-done.19) | copy-start | bytes 24580
  779.5 92.7 %all-to-all-start.2 = ((bf16[8,768,256]{2,0,1:T(8,128)(2,1)}), bf16[8,768,256]{2,0,1:T(8,128)(2,1)S(1)}, u32[]{:S(2)}, u32[]{:S(2)}) async-start(bf16[8,768,256]{2,0,1:T(8,128)(2,1)} %bitcast.129), calls=%async_computation.2 | async-start | bytes 6291456 | tf_op jit(solution)/shard_map/all_to_all | solution.py:140
  786.6 395.6 %reduce-scatter.4.cloned.1.call-start = ((), (), s32[]{:S(2)}) async-start(), calls=%async_computation.8 | async-start | bytes 9732096 | tf_op jit(solution)/shard_map/reduce_scatter | solution.py:152
  926.0 13.2 %copy-start.33 = (f32[768]{0:T(1024)S(1)}, f32[768]{0:T(1024)}, u32[]{:S(2)}) copy-start(f32[768]{0:T(1024)} %get-tuple-element.35) | copy-start | bytes 9220
  926.0 252.9 %copy-start.38 = (f32[96]{0:T(128)S(1)}, f32[96]{0:T(128)}, u32[]{:S(2)}) copy-start(f32[96]{0:T(128)} %param.18) | copy-start | bytes 1156
  926.0 252.9 %copy-start.39 = (f32[96]{0:T(128)S(1)}, f32[96]{0:T(128)}, u32[]{:S(2)}) copy-start(f32[96]{0:T(128)} %param.25) | copy-start | bytes 1156
  926.0 252.9 %copy-start.40 = (f32[96]{0:T(128)S(1)}, f32[96]{0:T(128)}, u32[]{:S(2)}) copy-start(f32[96]{0:T(128)} %param.24) | copy-start | bytes 1156
  926.0 253.5 %copy-start.29 = (f32[5,24]{1,0:T(8,128)S(1)}, f32[5,24]{1,0:T(8,128)}, u32[]{:S(2)}) copy-start(f32[5,24]{1,0:T(8,128)} %param.19) | copy-start | bytes 1444
  926.0 253.5 %copy-start.34 = (f32[5,24]{1,0:T(8,128)S(1)}, f32[5,24]{1,0:T(8,128)}, u32[]{:S(2)}) copy-start(f32[5,24]{1,0:T(8,128)} %param.27) | copy-start | bytes 1444
  926.0 253.5 %copy-start.35 = (f32[5,24]{1,0:T(8,128)S(1)}, f32[5,24]{1,0:T(8,128)}, u32[]{:S(2)}) copy-start(f32[5,24]{1,0:T(8,128)} %param.26) | copy-start | bytes 1444
  926.0 254.2 %copy-start.10 = (f32[96,768]{1,0:T(8,128)S(1)}, f32[96,768]{1,0:T(8,128)}, u32[]{:S(2)}) copy-start(f32[96,768]{1,0:T(8,128)} %param.17) | copy-start | bytes 884740
  926.0 254.2 %copy-start.13 = (f32[96,768]{1,0:T(8,128)S(1)}, f32[96,768]{1,0:T(8,128)}, u32[]{:S(2)}) copy-start(f32[96,768]{1,0:T(8,128)} %param.23) | copy-start | bytes 884740
  926.1 254.1 %copy-start.14 = (f32[96,768]{1,0:T(8,128)S(1)}, f32[96,768]{1,0:T(8,128)}, u32[]{:S(2)}) copy-start(f32[96,768]{1,0:T(8,128)} %param.22) | copy-start | bytes 884740
  926.1 256.1 %copy-start.12 = (f32[768,96]{0,1:T(8,128)S(1)}, f32[768,96]{0,1:T(8,128)}, u32[]{:S(2)}) copy-start(f32[768,96]{0,1:T(8,128)} %param.16) | copy-start | bytes 884740
  926.1 256.1 %copy-start.15 = (f32[768,96]{0,1:T(8,128)S(1)}, f32[768,96]{0,1:T(8,128)}, u32[]{:S(2)}) copy-start(f32[768,96]{0,1:T(8,128)} %param.21) | copy-start | bytes 884740
  926.1 256.1 %copy-start.16 = (f32[768,96]{0,1:T(8,128)S(1)}, f32[768,96]{0,1:T(8,128)}, u32[]{:S(2)}) copy-start(f32[768,96]{0,1:T(8,128)} %param.20) | copy-start | bytes 884740
  926.1 258.0 %all-to-all-start.3 = ((bf16[8,96,4096]{1,0,2:T(8,128)(2,1)}), bf16[8,96,4096]{1,0,2:T(8,128)(2,1)}, u32[]{:S(2)}, u32[]{:S(2)}) async-start(bf16[8,96,4096]{1,0,2:T(8,128)(2,1)} %copy.87), calls=%async_computation.3 | async-start | bytes 16777216 | tf_op jit(solution)/shard_map/all_to_all | solution.py:144
  (17 other events, 107.2 us)
Sparse Core Ops, SparseCore 0:
  51.9 145.1 all-gather.3
  407.8 88.7 all-gather.5
  715.3 169.5 reduce-scatter.5
  891.6 284.8 reduce-scatter.3
where the time goes:
time: 1240 us; the launch traced here: 1220 us
  blocking collectives  386 us (31%)
  other arithmetic  318 us (26%)
  matrix products  249 us (20%)
  local copies, waits for them, and re-layouts  150 us (12%)
  waiting for transfers between devices  69 us (6%)
  starting transfers between devices  34.8 us (3%)
  between operations  14.6 us (1%)
    unnamed x2, blocking collectives  281 us
    another operation x1, other arithmetic  271 us
    all_gather x1, blocking collectives, on_device(): lax.all_gather(norm_vec, ('seq', 'batch'), axis=1, tiled=True)  106 us
    all_to_all x1, waiting for transfers between devices, on_device(): piece = lax.all_to_all(dmix, 'seq', split_axis=1, concat_axis=2, tiled=True)  68.9 us
    dot_general x1, matrix products, on_device(): jnp.dot(hidden_low, first_low, preferred_element_type=jnp.float32)  64.9 us
    unnamed x92, local copies, waits for them, and re-layouts  42.6 us
    dot_general x1, matrix products, on_device(): jnp.einsum('lck,sdl->scdk', seq_tab, piece, preferred_element_type=jnp.fl...  34.3 us
    dot_general x1, matrix products, on_device(): jnp.einsum('lck,scdk->sdl', seq_tab, split, preferred_element_type=jnp.fl...  32.9 us
  transfers between devices with their start and end apart: 8, of which 1 were waited for; matrix products, arithmetic and copies ran while one was open for 50% of the time, Pallas kernels for 0%

commit v1 on v0

v1 whole, which is shorter than its diff:
```python
import functools
import math

import jax
import jax.numpy as jnp
import ml_dtypes
import numpy as np
from jax import lax
from jax.experimental import pallas as pl
from jax.experimental.pallas import tpu as pltpu
from jax.sharding import PartitionSpec as P

EPSILON = 1e-05
MOMENTUM = 0.9
AVG_DECAY = 0.9
RATE_MATRIX = 0.02
RATE_VECTOR = 0.1
LANES = 128
BLOCK = 256
MESH = pl.DeviceIdType.MESH
F32 = jnp.float32
BF16 = jnp.bfloat16


class Sizes:
    def __init__(self, parts, batch_parts, seqs, local, width, hidden):
        self.parts = parts
        self.batch_parts = batch_parts
        self.seqs = seqs
        self.local = local
        self.width = width
        self.hidden = hidden
        self.length = local * parts
        self.per = width // parts
        self.per_pad = -(-self.per // 16) * 16
        self.rows = self.per_pad + 16
        self.group = max(1, 512 // local)
        self.groups = seqs // self.group
        self.glen = self.group * local
        self.half = local // 2
        self.pack = max(1, LANES // self.half)
        self.depth = parts * LANES
        self.blocks = self.glen // BLOCK
        self.with_batch = batch_parts == 2
        self.seq_bits = parts.bit_length() - 1
        self.bits = self.seq_bits + (1 if self.with_batch else 0)
        self.shards = 1 << self.bits
        self.shard_rows = hidden // self.shards
        self.chunks = hidden // width
        self.chunk_shards = self.shards // self.chunks
        assert parts == 1 << self.seq_bits and self.half * self.pack == LANES
        assert self.group % self.pack == 0 and self.shard_rows % 16 == 0


def mixing_tables(z):
    width, per = z.width, z.per
    index = np.arange(width)
    angle = ((index[:, None] * index[None, :]) % width).astype(np.float32) * np.float32(
        2.0 * math.pi / width
    )
    cosine = np.cos(angle) / np.float32(math.sqrt(width))
    sine = np.sin(angle) / np.float32(math.sqrt(width))
    table = np.zeros((width + 16, width), np.float32)
    joined = np.zeros((width + 16, width), np.float32)
    for owner in range(z.parts):
        for slot in range(per):
            row, j = owner * per + slot, (owner // 2) * per + slot
            if owner % 2 == 0:
                table[row] = cosine[j]
                joined[row, j] = 1.0
                joined[row, (width - j) % width] = 1.0
            elif j > 0:
                table[row] = sine[j]
                joined[row, j] = -1.0
                joined[row, width - j] = 1.0
    table[width] = cosine[width // 2]
    joined[width, width // 2] = 1.0
    order = np.zeros((z.glen, z.glen), np.float32)
    row = 0
    for parity in range(2):
        for seq in range(z.group):
            for i in range(z.half):
                order[row, seq * z.local + 2 * i + parity] = 1.0
                row += 1
    low = ml_dtypes.bfloat16
    return table.astype(low), joined.astype(low), order.astype(low)


def sequence_tables(z):
    wave = (np.arange(z.length).astype(np.float32)) * np.float32(2.0 * math.pi / z.length)
    scale = np.float32(math.sqrt(z.length))
    waves = [
        (np.cos(wave) / scale).astype(ml_dtypes.bfloat16),
        (np.sin(wave) / scale).astype(ml_dtypes.bfloat16),
    ]
    source = np.arange(z.parts)[:, None, None] * z.local + 2 * np.arange(z.half)[None, None, :]
    source = np.broadcast_to(source, (z.parts, z.pack, z.half)).reshape(-1)
    out = np.arange(z.length // 2).reshape(z.parts // 2, z.local)
    result = np.empty((2, z.parts // 2, 2, z.depth, z.local), ml_dtypes.bfloat16)
    for parity in range(2):
        place = ((source + parity)[None, :, None] * out[:, None, :]) % z.length
        for kind in range(2):
            result[kind, :, parity] = waves[kind][place]
    return result


def dot(a, b):
    return jnp.dot(a, b, preferred_element_type=F32)


def dot_nt(a, b):
    return lax.dot_general(a, b, (((1,), (1,)), ((), ())), preferred_element_type=F32)


def dot_tn(a, b):
    return lax.dot_general(a, b, (((0,), (0,)), ((), ())), preferred_element_type=F32)


def normalize(value):
    center = value - jnp.mean(value, axis=-1, keepdims=True)
    spread = jnp.mean(center * center, axis=-1, keepdims=True)
    inverse = lax.rsqrt(spread + EPSILON)
    return center * inverse, inverse


def norm_backward(scaled, normed, inverse):
    return inverse * (
        scaled
        - jnp.mean(scaled, axis=-1, keepdims=True)
        - normed * jnp.mean(scaled * normed, axis=-1, keepdims=True)
    )


def gelu_and_slope(x):
    size = jnp.abs(x)
    t = 1.0 / (1.0 + (0.3275911 * math.sqrt(0.5)) * size)
    bell = jnp.exp(-0.5 * (x * x))
    poly = t * (
        0.5 * 0.254829592
        + t
        * (
            0.5 * -0.284496736
            + t * (0.5 * 1.421413741 + t * (0.5 * -1.453152027 + t * (0.5 * 1.061405429)))
        )
    )
    tail = poly * bell
    phi = jnp.where(x >= 0, 1.0 - tail, tail)
    return x * phi, phi + x * (bell * (1.0 / math.sqrt(2.0 * math.pi)))


KINDS = ("hidden", "gather", "seqmix", "feed", "scatter", "finish")


def plan(z):
    g = z.groups
    gathers = [("gather", i) for i in range(1, z.bits + 1)]
    scatters = [("scatter", i) for i in range(z.bits + 1)]
    steps = [("hidden", 0), gathers.pop(0), ("hidden", 1), gathers.pop(0), ("seqmix", 0)]
    for i in range(2, g):
        if gathers:
            steps.append(gathers.pop(0))
        steps += [("hidden", i), ("seqmix", i - 1)]
    steps += gathers
    back = 0
    for i in range(g):
        steps.append(("feed", i))
        if i == 0:
            steps.append(("seqmix", g - 1))
        if i >= 2:
            steps.append(("seqmix", g + back))
            back += 1
    steps.append(scatters.pop(0))
    done = 0
    while back < g:
        steps.append(("seqmix", g + back))
        back += 1
        if scatters:
            steps.append(scatters.pop(0))
        if done < back - 1:
            steps.append(("finish", done))
            done += 1
    while done < g:
        if scatters:
            steps.append(scatters.pop(0))
        steps.append(("finish", done))
        done += 1
    return steps + scatters


def step_kernel(
    z,
    x_hbm,
    cot_hbm,
    shard_in,
    shard_out,
    shard_vec,
    seq_table,
    table,
    joined,
    order,
    result_hbm,
    grad_hbm,
    total_in,
    total_out,
    total_vec,
    landed,
    full_in,
    full_out,
    full_vec,
    sum_in,
    sum_out,
    bias,
    vectors,
    vec_sum,
    vec_land,
    recv_a,
    recv_b,
    send,
    recv_sa,
    recv_sb,
    send_sa,
    send_sb,
    lhs,
    slots,
    source,
    xs,
    cs,
    act,
    slope,
    normed_one,
    hidden,
    low,
    dlow,
    work,
    stage,
    inverse_one,
    sem_a,
    sem_b,
    sem_send,
    sem_sa,
    sem_sb,
    sem_ssa,
    sem_ssb,
    sem_gather_send,
    sem_gather_recv,
    sem_scatter_send,
    sem_scatter_recv,
    sem_local,
    sem_slot,
):
    parts, per, groups = z.parts, z.per, z.groups
    me = lax.axis_index("seq")
    core = lax.axis_index("batch")
    fulls = (full_in, full_out, full_vec)
    sums = (sum_in, sum_out)
    vec_lanes = z.hidden + z.width

    own = [lax.rem(lax.div(me, 1 << (z.seq_bits - 1 - d)), 2) for d in range(z.seq_bits)]
    own += [core] if z.with_batch else []
    weights = [1 << (z.bits - 1 - d) for d in range(z.bits)]
    first = list(range(z.bits))
    second = list(first)
    a, b = z.seq_bits - 2, z.seq_bits - 1
    second[a], second[b] = second[b], second[a]
    gather_orders = (first, second, first)

    def partner(d):
        if d < z.seq_bits:
            return (me + (1 - 2 * own[d]) * (1 << (z.seq_bits - 1 - d)), core)
        return (me, 1 - core)

    def shard_at(free, k, flipped=None):
        index = 0
        for d in range(z.bits):
            if d in free:
                value = lax.rem(lax.div(k, 1 << free.index(d)), 2)
            elif d == flipped:
                value = 1 - own[d]
            else:
                value = own[d]
            index = index + value * weights[d]
        return index

    barrier = pltpu.get_barrier_semaphore()

    def greet(d, carry):
        pl.semaphore_signal(
            barrier, inc=1, device_id=(lax.rem(me + d, parts), core), device_id_type=MESH
        )
        return carry

    lax.fori_loop(1, parts, greet, 0)
    if z.with_batch:
        pl.semaphore_signal(barrier, inc=1, device_id=(me, 1 - core), device_id_type=MESH)
    greeted = parts - 1 + (1 if z.with_batch else 0)

    mine = shard_at((), 0)
    for w, shard in enumerate((shard_in, shard_out, shard_vec)):
        pltpu.make_async_copy(shard, fulls[w].at[mine], sem_local.at[w]).start()
    lhs[...] = jnp.zeros_like(lhs)
    send_sa[...] = jnp.zeros_like(send_sa)
    vec_sum[...] = jnp.zeros_like(vec_sum)

    @pl.when(me != 0)
    def _():
        recv_sa[...] = jnp.zeros_like(recv_sa)

    pl.semaphore_wait(barrier, greeted)

    def gather_send(stage_no):
        for w in range(3):
            order_w = gather_orders[w]
            free, d = order_w[:stage_no], order_w[stage_no]

            def body(k, carry, w=w, free=free, d=d):
                at = shard_at(free, k)
                pltpu.make_async_remote_copy(
                    src_ref=fulls[w].at[at],
                    dst_ref=fulls[w].at[at],
                    send_sem=sem_gather_send.at[w, stage_no],
                    recv_sem=sem_gather_recv.at[w, stage_no],
                    device_id=partner(d),
                    device_id_type=MESH,
                ).start()
                return carry

            lax.fori_loop(0, 1 << stage_no, body, 0)

    def gather_wait(stage_no):
        for w in range(3):
            some = fulls[w].at[pl.ds(0, 1 << stage_no)]
            pltpu.make_async_copy(some, some, sem_gather_recv.at[w, stage_no]).wait()

    def gather_done():
        for stage_no in range(z.bits):
            for w in range(3):
                some = fulls[w].at[pl.ds(0, 1 << stage_no)]
                pltpu.make_async_copy(some, some, sem_gather_send.at[w, stage_no]).wait()

    for w, shard in enumerate((shard_in, shard_out, shard_vec)):
        pltpu.make_async_copy(shard, fulls[w].at[mine], sem_local.at[w]).wait()
    gather_send(0)

    def gather_step(i):
        for stage_no in range(1, z.bits + 1):

            @pl.when(i == stage_no)
            def _(stage_no=stage_no):
                gather_wait(stage_no - 1)
                if stage_no < z.bits:
                    gather_send(stage_no)
                else:
                    gather_done()
                    place_vectors()

    def place_vectors():
        none = jnp.zeros((8, z.width - LANES), F32)
        lane = lax.broadcasted_iota(jnp.int32, (8, z.width), 1)
        wide = z.shard_rows
        narrow = z.width // z.shards
        for c in range(z.chunks):
            line = jnp.zeros((8, z.width), F32)
            for i in range(z.chunk_shards):
                row = jnp.concatenate([full_vec[c * z.chunk_shards + i, 0:8], none], axis=1)
                row = jnp.where(lane < wide, row, 0.0)
                line = line + (pltpu.roll(row, i * wide, 1) if i else row)
            bias[:, c * z.width : (c + 1) * z.width] = line[0:1]
        line = jnp.zeros((8, z.width), F32)
        for i in range(z.shards):
            row = jnp.concatenate([full_vec[i, 8:16], none], axis=1)
            row = jnp.where(lane < narrow, row, 0.0)
            line = line + (pltpu.roll(row, i * narrow, 1) if i else row)
        vectors[...] = line

    def wait_all(ref, sem):
        pltpu.make_async_copy(ref, ref, sem).wait()

    def wait_sent(g):
        some = send.at[g, pl.ds(0, parts - 1)]
        pltpu.make_async_copy(some, some, sem_send.at[g]).wait()

    def push(g, peer, landing, sem):
        @pl.when(peer != me)
        def _():
            pltpu.make_async_remote_copy(
                src_ref=send.at[g, peer],
                dst_ref=landing.at[g, me],
                send_sem=sem_send.at[g],
                recv_sem=sem.at[g],
                device_id=(peer, core),
                device_id_type=MESH,
            ).start()

        @pl.when(peer == me)
        def _():
            pltpu.make_async_copy(send.at[g, me], landing.at[g, me], sem.at[g]).start()

    def hidden_step(u):
        g = lax.rem(u, groups)
        tokens = pl.ds(pl.multiple_of(g * z.glen, z.glen), z.glen)

        @pl.when(u < groups)
        def _():
            copy = pltpu.make_async_copy(x_hbm.at[tokens], source, sem_local.at[3])
            copy.start()
            copy.wait()

        moved = dot(order[...], source[...]).astype(BF16)
        out = dot_nt(table[...], moved)

        @pl.when(u >= groups)
        def _():
            wait_sent(g)

            @pl.when(me != 0)
            def _():
                wait_all(send_sa.at[g], sem_ssa.at[g])

        send[g] = out[: z.width].reshape(parts, per, z.glen).astype(BF16)
        last = out[z.width : z.width + 1].astype(BF16).astype(F32)
        for r in range(z.glen // LANES):
            send_sa[g, r : r + 1, :] = last[:, r * LANES : (r + 1) * LANES]

        @pl.when(me != 0)
        def _():
            pltpu.make_async_remote_copy(
                src_ref=send_sa.at[g],
                dst_ref=recv_sa.at[g, me],
                send_sem=sem_ssa.at[g],
                recv_sem=sem_sa.at[g],
                device_id=(0, core),
                device_id_type=MESH,
            ).start()

        @pl.when(me == 0)
        def _():
            pltpu.make_async_copy(send_sa.at[g], recv_sa.at[g, 0], sem_sa.at[g]).start()

        def body(d, carry):
            push(g, lax.rem(me + d, parts), recv_a, sem_a)
            return carry

        lax.fori_loop(0, parts, body, 0)

    def seqmix_step(u):
        g = lax.rem(u, groups)
        kind = lax.rem(me, 2)
        half_parts = parts // 2

        def fetch(j):
            which = lax.rem(me + j, half_parts)
            return pltpu.make_async_copy(
                seq_table.at[kind, which], slots.at[lax.rem(j, 2)], sem_slot.at[lax.rem(j, 2)]
            )

        fetch(0).start()
        wait_all(recv_a.at[g], sem_a.at[g])

        @pl.when(me == 0)
        def _():
            wait_all(recv_sa.at[g], sem_sa.at[g])

        def gather_rows(c, carry):
            columns = pl.ds(pl.multiple_of(c * LANES, LANES), LANES)
            for parity in range(2):
                for s in range(z.group):
                    at = parity * (z.group // z.pack) + s // z.pack
                    rows = recv_a[g, c, :, at * LANES : (at + 1) * LANES]
                    line = jnp.broadcast_to(recv_sa[g, c, at : at + 1, :], (16, LANES)).astype(BF16)
                    if z.pack > 1:
                        lane = lax.broadcasted_iota(jnp.int32, (per, LANES), 1) // z.half
                        rows = jnp.where(lane == s % z.pack, rows.astype(F32), 0.0).astype(BF16)
                        lane = lax.broadcasted_iota(jnp.int32, (16, LANES), 1) // z.half
                        line = jnp.where(lane == s % z.pack, line.astype(F32), 0.0).astype(BF16)
                    lhs[parity, s, 0:per, columns] = rows
                    lhs[parity, s, z.per_pad : z.rows, columns] = line
            return carry

        lax.fori_loop(0, parts, gather_rows, 0)
        wait_sent(g)

        @pl.when((me == 0) & (u >= groups))
        def _():
            some = send_sb.at[g, pl.ds(0, parts - 1)]
            pltpu.make_async_copy(some, some, sem_ssb.at[g]).wait()

        def body(j, carry):
            @pl.when(j + 1 < half_parts)
            def _():
                fetch(j + 1).start()

            fetch(j).wait()
            slot = lax.rem(j, 2)
            near = lax.rem(me + j, half_parts)
            even = dot(lhs[0].reshape(z.group * z.rows, z.depth), slots[slot, 0])
            odd = dot(lhs[1].reshape(z.group * z.rows, z.depth), slots[slot, 1])
            for peer, value in ((near, even + odd), (near + half_parts, even - odd)):
                value = value.reshape(z.group, z.rows, z.local)
                for s in range(z.group):
                    lanes = slice(s * z.local, (s + 1) * z.local)
                    send[g, peer, :, lanes] = value[s, :per].astype(BF16)
                    for r in range(z.local // LANES):
                        at = s * (z.local // LANES) + r
                        send_sb[g, peer, at : at + 1, :] = value[
                            s, z.per_pad : z.per_pad + 1, r * LANES : (r + 1) * LANES
                        ]
                push(g, peer, recv_b, sem_b)

                @pl.when((me == 0) & (peer != 0))
                def _(peer=peer):
                    pltpu.make_async_remote_copy(
                        src_ref=send_sb.at[g, peer],
                        dst_ref=recv_sb.at[g],
                        send_sem=sem_ssb.at[g],
                        recv_sem=sem_sb.at[g],
                        device_id=(peer, core),
                        device_id_type=MESH,
                    ).start()

                @pl.when((me == 0) & (peer == 0))
                def _():
                    pltpu.make_async_copy(send_sb.at[g, 0], recv_sb.at[g], sem_sb.at[g]).start()

            return carry

        lax.fori_loop(0, half_parts, body, 0)

    def mixed_block(g, t):
        lanes = pl.ds(pl.multiple_of(t * BLOCK, BLOCK), BLOCK)
        rows = recv_b[g, :, :, lanes]
        if per % 16:
            rows = rows.astype(F32).reshape(z.width, BLOCK).astype(BF16)
        else:
            rows = rows.reshape(z.width, BLOCK)
        line = jnp.concatenate(
            [recv_sb[g, pl.ds(t * (BLOCK // LANES) + r, 1), :] for r in range(BLOCK // LANES)], axis=1
        )
        line = jnp.broadcast_to(line, (16, BLOCK)).astype(BF16)
        return dot_tn(rows, joined[: z.width]) + dot_tn(line, joined[z.width :])

    def mixed_wait(g):
        wait_all(recv_b.at[g], sem_b.at[g])
        wait_all(recv_sb.at[g], sem_sb.at[g])

    def feed_step(g):
        tokens = pl.ds(pl.multiple_of(g * z.glen, z.glen), z.glen)
        load_x = pltpu.make_async_copy(x_hbm.at[tokens], xs, sem_local.at[4])
        load_c = pltpu.make_async_copy(cot_hbm.at[tokens], cs, sem_local.at[5])
        load_x.start()
        load_c.start()
        mixed_wait(g)
        load_x.wait()
        load_c.wait()

        def block(t, carry):
            rows = pl.ds(pl.multiple_of(t * BLOCK, BLOCK), BLOCK)
            outer = pl.ds(pl.multiple_of(g * z.glen + t * BLOCK, BLOCK), BLOCK)
            value = xs[rows, :].astype(F32) + mixed_block(g, t)
            normed, inverse = normalize(value)
            normed_one[...] = normed
            inverse_one[...] = inverse
            value = normed * vectors[0:1, :] + vectors[1:2, :]
            hidden[...] = value
            low[...] = value.astype(BF16)
            work[...] = jnp.zeros_like(work)

            def forward(c, carry):
                lanes = pl.ds(pl.multiple_of(c * z.width, z.width), z.width)
                some = pl.ds(c * z.chunk_shards, z.chunk_shards)
                pre = dot_nt(low[...], full_in[some].reshape(z.width, z.width)) + bias[:, lanes]
                value, pull = gelu_and_slope(pre)
                value = value.astype(BF16)
                act[:, lanes] = value
                slope[:, lanes] = pull.astype(BF16)
                work[...] += dot(value, full_out[some].reshape(z.width, z.width))
                return carry

            lax.fori_loop(0, z.chunks, forward, 0)
            normed, inverse = normalize(hidden[...] + (work[...] + vectors[4:5, :]))
            stage[...] = normed * vectors[2:3, :] + vectors[3:4, :]
            put = pltpu.make_async_copy(stage, result_hbm.at[outer], sem_local.at[6])
            put.start()
            grad = cs[rows, :].astype(F32)
            here = pl.ds(z.hidden, z.width)
            vec_sum[2:3, here] += jnp.sum(grad * normed, axis=0, keepdims=True)
            vec_sum[3:4, here] += jnp.sum(grad, axis=0, keepdims=True)
            grad = norm_backward(grad * vectors[2:3, :], normed, inverse)
            work[...] = grad
            dffo = grad.astype(BF16)
            dlow[...] = dffo
            vec_sum[4:5, here] += jnp.sum(dffo.astype(F32), axis=0, keepdims=True)

            def backward(c, carry):
                lanes = pl.ds(pl.multiple_of(c * z.width, z.width), z.width)
                some = pl.ds(c * z.chunk_shards, z.chunk_shards)
                shape = (z.chunk_shards, z.shard_rows, z.width)
                dpre = dot_nt(dlow[...], full_out[some].reshape(z.width, z.width))
                dpre = (dpre * slope[:, lanes].astype(F32)).astype(BF16)
                vec_sum[0:1, lanes] += jnp.sum(dpre.astype(F32), axis=0, keepdims=True)
                work[...] += dot(dpre, full_in[some].reshape(z.width, z.width))
                into_out = dot_tn(act[:, lanes], dlow[...]).reshape(shape)
                into_in = dot_tn(dpre, low[...]).reshape(shape)

                @pl.when(g + t == 0)
                def _():
                    sum_out[some] = into_out
                    sum_in[some] = into_in

                @pl.when(g + t > 0)
                def _():
                    sum_out[some] += into_out
                    sum_in[some] += into_in

                return carry

            lax.fori_loop(0, z.chunks, backward, 0)
            grad, normed = work[...], normed_one[...]
            vec_sum[0:1, here] += jnp.sum(grad * normed, axis=0, keepdims=True)
            vec_sum[1:2, here] += jnp.sum(grad, axis=0, keepdims=True)
            grad = norm_backward(grad * vectors[0:1, :], normed, inverse_one[...])
            source[rows, :] = grad.astype(BF16)
            put.wait()
            stage[...] = grad
            put = pltpu.make_async_copy(stage, grad_hbm.at[outer], sem_local.at[6])
            put.start()
            put.wait()
            return carry

        lax.fori_loop(0, z.blocks, block, 0)
        hidden_step(g + groups)

    def finish_step(g):
        def load(t):
            outer = pl.ds(pl.multiple_of(g * z.glen + t * BLOCK, BLOCK), BLOCK)
            return pltpu.make_async_copy(grad_hbm.at[outer], work, sem_local.at[7])

        load(0).start()
        mixed_wait(g)

        def block(t, carry):
            outer = pl.ds(pl.multiple_of(g * z.glen + t * BLOCK, BLOCK), BLOCK)

            @pl.when(t > 0)
            def _():
                load(t).start()

            value = mixed_block(g, t)
            load(t).wait()
            stage[...] = work[...] + value
            put = pltpu.make_async_copy(stage, grad_hbm.at[outer], sem_local.at[6])
            put.start()
            put.wait()
            return carry

        lax.fori_loop(0, z.blocks, block, 0)

    offsets = [sum(1 << (z.bits - 1 - i) for i in range(s)) for s in range(z.bits)]

    def scatter_orders(w):
        if w < 2:
            return gather_orders[w][::-1]
        return gather_orders[0][::-1]

    def scatter_send(s):
        count = 1 << (z.bits - 1 - s)
        for w in range(2):
            path = scatter_orders(w)
            d, free = path[s], path[s + 1 :]

            def body(k, carry, w=w, d=d, free=free):
                at = shard_at(free, k, flipped=d)
                fulls[w][at] = sums[w][at].astype(BF16)
                pltpu.make_async_remote_copy(
                    src_ref=fulls[w].at[at],
                    dst_ref=landed.at[w, offsets[s] + k],
                    send_sem=sem_scatter_send.at[w, s],
                    recv_sem=sem_scatter_recv.at[w, s],
                    device_id=partner(d),
                    device_id_type=MESH,
                ).start()
                return carry

            lax.fori_loop(0, count, body, 0)
        pltpu.make_async_remote_copy(
            src_ref=vec_sum,
            dst_ref=vec_land.at[s],
            send_sem=sem_scatter_send.at[2, s],
            recv_sem=sem_scatter_recv.at[2, s],
            device_id=partner(scatter_orders(2)[s]),
            device_id_type=MESH,
        ).start()

    def scatter_add(s):
        count = 1 << (z.bits - 1 - s)
        for w in range(2):
            path = scatter_orders(w)
            free = path[s + 1 :]
            some = landed.at[w, pl.ds(offsets[s], count)]
            wait_all(some, sem_scatter_recv.at[w, s])

            def fetch(k, carry, w=w, free=free):
                pltpu.make_async_copy(
                    landed.at[w, offsets[s] + k], fulls[w].at[shard_at(free, k)], sem_local.at[w]
                ).start()
                return carry

            lax.fori_loop(0, count, fetch, 0)
        wait_all(vec_sum, sem_scatter_send.at[2, s])
        wait_all(vec_land.at[s], sem_scatter_recv.at[2, s])
        vec_sum[...] += vec_land[s]
        for w in range(2):
            free = scatter_orders(w)[s + 1 :]
            some = landed.at[w, pl.ds(offsets[s], count)]
            wait_all(some, sem_local.at[w])

            def add(k, carry, w=w, free=free):
                at = shard_at(free, k)
                sums[w][at] += fulls[w][at].astype(F32)
                return carry

            lax.fori_loop(0, count, add, 0)

    def scatter_step(i):
        for s in range(z.bits + 1):

            @pl.when(i == s)
            def _(s=s):
                if s > 0:
                    scatter_add(s - 1)
                if s < z.bits:
                    scatter_send(s)

    steps = plan(z)
    bodies = (hidden_step, gather_step, seqmix_step, feed_step, scatter_step, finish_step)

    def one_step(s, carry):
        kind, argument = 0, 0
        for i, (name, value) in enumerate(steps):
            here = (s == i).astype(jnp.int32)
            kind = kind + here * KINDS.index(name)
            argument = argument + here * value
        for k, body in enumerate(bodies):

            @pl.when(kind == k)
            def _(body=body):
                body(argument)

        return carry

    lax.fori_loop(0, len(steps), one_step, 0)

    for w, total in ((0, total_in), (1, total_out)):
        pltpu.make_async_copy(sums[w].at[mine], total, sem_local.at[w]).start()
    pltpu.make_async_copy(vec_sum, total_vec, sem_local.at[2]).start()
    for g in range(groups):
        wait_sent(g)

        @pl.when(me != 0)
        def _(g=g):
            wait_all(send_sa.at[g], sem_ssa.at[g])

        @pl.when(me == 0)
        def _(g=g):
            some = send_sb.at[g, pl.ds(0, parts - 1)]
            pltpu.make_async_copy(some, some, sem_ssb.at[g]).wait()

    for s in range(z.bits):
        for w in range(2):
            some = landed.at[w, pl.ds(offsets[s], 1 << (z.bits - 1 - s))]
            wait_all(some, sem_scatter_send.at[w, s])
    for w, total in ((0, total_in), (1, total_out)):
        pltpu.make_async_copy(sums[w].at[mine], total, sem_local.at[w]).wait()
    pltpu.make_async_copy(vec_sum, total_vec, sem_local.at[2]).wait()


def run_step(z, x, cot, shard_in, shard_out, shard_vec, tables):
    tokens = z.seqs * z.local
    vec_lanes = z.hidden + z.width
    shard = (z.shards, z.shard_rows, z.width)
    block = (BLOCK, z.width)
    any_space, vmem = pl.BlockSpec(memory_space=pl.ANY), pl.BlockSpec(memory_space=pltpu.VMEM)
    dma = pltpu.SemaphoreType.DMA
    g = z.groups
    scratch = [
        pltpu.VMEM(shard, BF16),
        pltpu.VMEM(shard, BF16),
        pltpu.VMEM((z.shards, 16, LANES), F32),
        pltpu.VMEM(shard, F32),
        pltpu.VMEM(shard, F32),
        pltpu.VMEM((1, z.hidden), F32),
        pltpu.VMEM((8, z.width), F32),
        pltpu.VMEM((8, vec_lanes), F32),
        pltpu.VMEM((z.bits, 8, vec_lanes), F32),
        pltpu.VMEM((g, z.parts, z.per, z.glen), BF16),
        pltpu.VMEM((g, z.parts, z.per, z.glen), BF16),
        pltpu.VMEM((g, z.parts, z.per, z.glen), BF16),
        pltpu.VMEM((g, z.parts, 8, LANES), F32),
        pltpu.VMEM((g, 8, LANES), F32),
        pltpu.VMEM((g, 8, LANES), F32),
        pltpu.VMEM((g, z.parts, 8, LANES), F32),
        pltpu.VMEM((2, z.group, z.rows, z.depth), BF16),
        pltpu.VMEM((2, 2, z.depth, z.local), BF16),
        pltpu.VMEM((z.glen, z.width), BF16),
        pltpu.VMEM((z.glen, z.width), BF16),
        pltpu.VMEM((z.glen, z.width), BF16),
        pltpu.VMEM((BLOCK, z.hidden), BF16),
        pltpu.VMEM((BLOCK, z.hidden), BF16),
        pltpu.VMEM(block, F32),
        pltpu.VMEM(block, F32),
        pltpu.VMEM(block, BF16),
        pltpu.VMEM(block, BF16),
        pltpu.VMEM(block, F32),
        pltpu.VMEM(block, F32),
        pltpu.VMEM((BLOCK, 1), F32),
        dma((g,)),
        dma((g,)),
        dma((g,)),
        dma((g,)),
        dma((g,)),
        dma((g,)),
        dma((g,)),
        dma((3, z.bits)),
        dma((3, z.bits)),
        dma((3, z.bits)),
        dma((3, z.bits)),
        dma((8,)),
        dma((2,)),
    ]
    return pl.pallas_call(
        functools.partial(step_kernel, z),
        out_shape=(
            jax.ShapeDtypeStruct((tokens, z.width), F32),
            jax.ShapeDtypeStruct((tokens, z.width), F32),
            jax.ShapeDtypeStruct(shard[1:], F32),
            jax.ShapeDtypeStruct(shard[1:], F32),
            jax.ShapeDtypeStruct((8, vec_lanes), F32),
            jax.ShapeDtypeStruct((2, z.shards - 1) + shard[1:], BF16),
        ),
        in_specs=[any_space] * 6 + [vmem] * 3,
        out_specs=(any_space,) * 6,
        scratch_shapes=scratch,
        compiler_params=pltpu.CompilerParams(
            collective_id=0, has_side_effects=True, vmem_limit_bytes=64 << 20
        ),
        cost_estimate=pl.CostEstimate(
            flops=12 * tokens * z.width * z.hidden + 16 * tokens * z.width * z.length // 16,
            bytes_accessed=40 * tokens * z.width,
            transcendentals=tokens * z.hidden,
        ),
    )(x, cot, shard_in, shard_out, shard_vec, *tables)


def nesterov(weight, moment, average, grad, rate, scale):
    scaled = grad * scale
    moment_new = MOMENTUM * moment + scaled
    weight_new = weight - rate * (scaled + MOMENTUM * moment_new)
    average_new = AVG_DECAY * average + (1.0 - AVG_DECAY) * weight_new
    return (moment_new, weight_new, average_new)


def on_device(
    seq_parts,
    batch_parts,
    layer_input_tokens,
    cotangent,
    weight_in,
    weight_out,
    bias_ff,
    norm_vec,
    moment_in,
    average_in,
    moment_out,
    average_out,
    moment_bias,
    average_bias,
    moment_norm,
    average_norm,
):
    seqs, local, width = layer_input_tokens.shape
    devices = seq_parts * batch_parts
    hidden = weight_out.shape[0] * devices
    z = Sizes(seq_parts, batch_parts, seqs, local, width, hidden)
    tokens = seqs * local

    shard_in = weight_in.T.astype(BF16)
    shard_out = weight_out.astype(BF16)
    bias_shard, norm_shard = bias_ff, norm_vec
    if not z.with_batch:
        shard_in, shard_out, bias_shard = (
            lax.all_gather(v, "batch", axis=0, tiled=True) for v in (shard_in, shard_out, bias_shard)
        )
        norm_shard = lax.all_gather(norm_shard, "batch", axis=1, tiled=True)
    bias_line = jnp.pad(bias_shard[None, :], ((0, 7), (0, LANES - bias_shard.shape[0])))
    norm_rows = jnp.pad(norm_shard, ((0, 3), (0, LANES - norm_shard.shape[1])))
    shard_vec = jnp.concatenate([bias_line, norm_rows], axis=0)

    tables = [jnp.asarray(sequence_tables(z))] + [jnp.asarray(t) for t in mixing_tables(z)]
    result, tokens_grad, grad_in, grad_out, grad_vec, _ = run_step(
        z,
        layer_input_tokens.reshape(tokens, width),
        cotangent.reshape(tokens, width),
        shard_in,
        shard_out,
        shard_vec,
        tables,
    )
    index = lax.axis_index("seq") * batch_parts + lax.axis_index("batch")
    if not z.with_batch:
        grad_in = lax.psum_scatter(grad_in, "batch", scatter_dimension=0, tiled=True)
        grad_out = lax.psum_scatter(grad_out, "batch", scatter_dimension=0, tiled=True)
        grad_vec = lax.psum(grad_vec, "batch")
    count, narrow = hidden // devices, width // devices
    grad_bias = lax.dynamic_slice(grad_vec[0], (index * count,), (count,))
    grad_norm = lax.dynamic_slice(grad_vec[:5], (0, hidden + index * narrow), (5, narrow))

    scale = (seqs * batch_parts * local * seq_parts) ** (-0.5)
    m_in, w_in_new, a_in = nesterov(
        weight_in, moment_in, average_in, grad_in.T, RATE_MATRIX, scale
    )
    m_out, w_out_new, a_out = nesterov(
        weight_out, moment_out, average_out, grad_out, RATE_MATRIX, scale
    )
    m_bias, b_new, a_bias = nesterov(
        bias_ff, moment_bias, average_bias, grad_bias, RATE_VECTOR, scale
    )
    m_norm, n_new, a_norm = nesterov(
        norm_vec, moment_norm, average_norm, grad_norm, RATE_VECTOR, scale
    )
    return (
        result.reshape(seqs, local, width),
        tokens_grad.reshape(seqs, local, width),
        m_in,
        w_in_new,
        a_in,
        m_out,
        w_out_new,
        a_out,
        m_bias,
        b_new,
        a_bias,
        m_norm,
        n_new,
        a_norm,
    )


def solution(mesh):
    tokens = P("batch", "seq", None)
    columns, rows, flat = P(None, ("seq", "batch")), P(("seq", "batch"), None), P(("seq", "batch"))
    return jax.shard_map(
        functools.partial(on_device, mesh.shape["seq"], mesh.shape["batch"]),
        mesh=mesh,
        in_specs=(tokens, tokens, columns, rows, flat, columns)
        + (columns, columns, rows, rows, flat, flat, columns, columns),
        out_specs=(tokens, tokens)
        + (columns,) * 3
        + (rows,) * 3
        + (flat,) * 3
        + (columns,) * 3,
        check_vma=False,
    )
```

time: 1240 us -> 434 us (0.35); the launches traced: 1220 us -> 432 us
  Pallas kernels: 0 us -> 410 us
  blocking collectives: 386 us -> 0 us
  other arithmetic: 318 us -> 11.9 us
  matrix products: 249 us -> 0 us
  local copies, waits for them, and re-layouts: 150 us -> 9.72 us
  waiting for transfers between devices: 69 us -> 0 us
  starting transfers between devices: 34.8 us -> 0 us
  between operations: 14.6 us -> 0.66 us
    pallas_call x0 -> x1, Pallas kernels: none -> 410 us  [run_step(): pl.pallas_call(functools.partial(step_kernel, z), out_shape=(jax.ShapeDty...]
    unnamed x2 -> x0, blocking collectives: 281 us -> none
    another operation x1 -> x0, other arithmetic: 271 us -> none
    dot_general x10 -> x0, matrix products: 249 us -> none  [the longest x1 64.9 us: on_device(): jnp.dot(hidden_low, first_low, preferred_element_type=jnp.float32)]
    all_gather x1 -> x0, blocking collectives: 106 us -> none  [on_device(): lax.all_gather(norm_vec, ('seq', 'batch'), axis=1, tiled=True)]
    all_to_all x4 -> x0, waiting for transfers between devices: 68.9 us -> none  [the longest x1 68.9 us: on_device(): piece = lax.all_to_all(dmix, 'seq', split_axis=1, concat_axis=2, tiled=True)]
    convert_element_type x5 -> x0, local copies, waits for them, and re-layouts: 40.8 us -> none  [the longest x1 17.1 us: on_device(): both = jnp.einsum('gmn,nr->grm', layer_input_tokens, hidden_trig_lookup,...]
    all_to_all x5 -> x0, local copies, waits for them, and re-layouts: 36.8 us -> none  [the longest x1 11.8 us: on_device(): lax.all_to_all(dboth_slices, 'seq', split_axis=2, concat_axis=1, tiled=True)]
  transfers between devices with their start and end apart: 8 -> 0, of which waited for: 1 -> 0; matrix products, arithmetic and copies ran while one was open for 50% -> 0% of each run, Pallas kernels for 0% -> 0%
where the time goes in v1:
time: 434 us; the launch traced here: 432 us
  Pallas kernels  410 us (94%)
  other arithmetic  11.9 us (3%)
  local copies, waits for them, and re-layouts  9.72 us (2%)
    pallas_call x1, Pallas kernels, run_step(): pl.pallas_call(functools.partial(step_kernel, z), out_shape=(jax.ShapeDty...  410 us
    unnamed x6, local copies, waits for them, and re-layouts  8.81 us

profile of v1, /device:TPU:24, one launch (start us, length us, event | category | flops | bytes accessed | tf_op | source)
XLA Modules:
  0.0 432.2 jit_solution(10748210829361553615)
XLA Ops:
  0.6 1.6 convert_bitcast_fusion.shard_in
  2.3 1.6 convert_element_type.14.shard_out
  3.9 1.3 select_maximum_fusion.shard_vec
  5.2 410.0 %shard_map.281 = (f32[2048,768]{1,0:T(8,128)}, f32[2048,768]{1,0:T(8,128)}, f32[96,768]{1,0:T(8,128)}, f32[96,768]{1,0:T(8,128)}, f32[8,3840]{1,0:T(8,128)}, /*index=5*/bf16[2,31,96,768]{3,2,1,0:T(8,128)(2,1)}) custom-call(bf16[2048,768]{1,0:T(8,128)(2,1)} %bitcast.32, bf16[2048,768]{1,0:T(8,128)(2,1)} %bitcast.33, ...), custom_call_target="tpu_custom_call" | custom-call | flops 64424509440 | bytes 62914560 | tf_op jit(solution)/shard_map/pallas_call | solution.py:829
  415.2 2.2 multiply_add_fusion.2
  417.4 0.0 slice-start
  417.4 2.4 multiply_add_fusion
  419.8 0.9 slice.6
  420.7 1.3 multiply_add_fusion.5
  422.0 1.4 multiply_add_fusion.3
  423.4 0.0 slice-start.1
  423.4 6.1 %copy.34 = f32[8,256,768]{2,1,0:T(8,128)} copy(f32[8,256,768]{2,1,0:T(8,128)} %bitcast.29) | data formatting | bytes 12582912
  429.5 0.0 slice-done
  429.5 0.0 slice-done.1
  429.5 2.7 copy.35
  (1 shorter events, 0.0 us)
Async XLA Ops:
  417.4 12.1 %slice-start = ((s8[6291456]{0:T(1024)(128)(4,1)}), s8[2097152]{0:T(1024)(128)(4,1)S(1)}, s32[]{:S(2)}) async-start(s8[6291456]{0:T(1024)(128)(4,1)} %bitcast.26), calls=%async_computation | async-start | bytes 4194304
  423.4 6.1 %slice-start.1 = ((s8[6291456]{0:T(1024)(128)(4,1)}), s8[4194304]{0:T(1024)(128)(4,1)S(1)}, s32[]{:S(2)}) async-start(s8[6291456]{0:T(1024)(128)(4,1)} %bitcast.26), calls=%async_computation.1 | async-start | bytes 8388608

commit v2 on v1

--- a/solution.py
+++ b/solution.py
@@ -16,7 +16,6 @@
 RATE_MATRIX = 0.02
 RATE_VECTOR = 0.1
 LANES = 128
-BLOCK = 256
 MESH = pl.DeviceIdType.MESH
 F32 = jnp.float32
 BF16 = jnp.bfloat16
@@ -40,7 +39,10 @@
         self.half = local // 2
         self.pack = max(1, LANES // self.half)
         self.depth = parts * LANES
-        self.blocks = self.glen // BLOCK
+        self.pair = 2 if self.groups % 2 == 0 and self.depth <= 2048 else 1
+        self.pairs = self.groups // self.pair
+        self.lhs_rows = 2 * self.pair * self.group * self.rows
+        self.shared = self.lhs_rows <= self.glen and self.depth <= hidden
         self.with_batch = batch_parts == 2
         self.seq_bits = parts.bit_length() - 1
         self.bits = self.seq_bits + (1 if self.with_batch else 0)
@@ -148,43 +150,26 @@
     return x * phi, phi + x * (bell * (1.0 / math.sqrt(2.0 * math.pi)))
 
 
-KINDS = ("hidden", "gather", "seqmix", "feed", "scatter", "finish")
+STEPS = {"H": "hidden", "G": "gather", "T": "pair", "t": "single", "F": "feed", "S": "scatter", "E": "finish"}
+KINDS = tuple(STEPS.values())
+
+
+ORDER = (
+    "G1", "H0", "G2", "H1", "G3", "H2", "H3", "T0", "G4", "T1", "G5",
+    "F0", "F1", "F2", "T2", "F3", "S0", "t6", "S1", "S2", "t7", "E0",
+    "S3", "E1", "E2", "S4", "E3", "S5",
+)
 
 
 def plan(z):
+    if (z.groups, z.pairs, z.bits) == (4, 2, 5):
+        return [(STEPS[name[0]], int(name[1:])) for name in ORDER]
     g = z.groups
-    gathers = [("gather", i) for i in range(1, z.bits + 1)]
-    scatters = [("scatter", i) for i in range(z.bits + 1)]
-    steps = [("hidden", 0), gathers.pop(0), ("hidden", 1), gathers.pop(0), ("seqmix", 0)]
-    for i in range(2, g):
-        if gathers:
-            steps.append(gathers.pop(0))
-        steps += [("hidden", i), ("seqmix", i - 1)]
-    steps += gathers
-    back = 0
-    for i in range(g):
-        steps.append(("feed", i))
-        if i == 0:
-            steps.append(("seqmix", g - 1))
-        if i >= 2:
-            steps.append(("seqmix", g + back))
-            back += 1
-    steps.append(scatters.pop(0))
-    done = 0
-    while back < g:
-        steps.append(("seqmix", g + back))
-        back += 1
-        if scatters:
-            steps.append(scatters.pop(0))
-        if done < back - 1:
-            steps.append(("finish", done))
-            done += 1
-    while done < g:
-        if scatters:
-            steps.append(scatters.pop(0))
-        steps.append(("finish", done))
-        done += 1
-    return steps + scatters
+    steps = [("hidden", i) for i in range(g)] + [("gather", i) for i in range(1, z.bits + 1)]
+    steps += [("single", i) for i in range(g)] + [("feed", i) for i in range(g)]
+    steps += [("scatter", 0)] + [("single", g + i) for i in range(g)]
+    steps += [("scatter", i) for i in range(1, z.bits + 1)]
+    return steps + [("finish", i) for i in range(g)]
 
 
 def step_kernel(
@@ -220,15 +205,13 @@
     recv_sb,
     send_sa,
     send_sb,
-    lhs,
+    own_lhs,
     slots,
     source,
-    xs,
     cs,
     act,
     slope,
     normed_one,
-    hidden,
     low,
     dlow,
     work,
@@ -253,7 +236,7 @@
     core = lax.axis_index("batch")
     fulls = (full_in, full_out, full_vec)
     sums = (sum_in, sum_out)
-    vec_lanes = z.hidden + z.width
+    lhs = act if z.shared else own_lhs
 
     own = [lax.rem(lax.div(me, 1 << (z.seq_bits - 1 - d)), 2) for d in range(z.seq_bits)]
     own += [core] if z.with_batch else []
@@ -297,7 +280,6 @@
     mine = shard_at((), 0)
     for w, shard in enumerate((shard_in, shard_out, shard_vec)):
         pltpu.make_async_copy(shard, fulls[w].at[mine], sem_local.at[w]).start()
-    lhs[...] = jnp.zeros_like(lhs)
     send_sa[...] = jnp.zeros_like(send_sa)
     vec_sum[...] = jnp.zeros_like(vec_sum)
 
@@ -442,217 +424,228 @@
 
         lax.fori_loop(0, parts, body, 0)
 
-    def seqmix_step(u):
-        g = lax.rem(u, groups)
-        kind = lax.rem(me, 2)
-        half_parts = parts // 2
-
-        def fetch(j):
-            which = lax.rem(me + j, half_parts)
-            return pltpu.make_async_copy(
-                seq_table.at[kind, which], slots.at[lax.rem(j, 2)], sem_slot.at[lax.rem(j, 2)]
-            )
-
-        fetch(0).start()
-        wait_all(recv_a.at[g], sem_a.at[g])
-
-        @pl.when(me == 0)
-        def _():
-            wait_all(recv_sa.at[g], sem_sa.at[g])
-
-        def gather_rows(c, carry):
-            columns = pl.ds(pl.multiple_of(c * LANES, LANES), LANES)
+    half_parts = parts // 2
+    deep = z.depth // 2
+
+    def fetch(j, quarter):
+        return pltpu.make_async_copy(
+            seq_table.at[
+                lax.rem(me, 2),
+                lax.rem(me + j, half_parts),
+                quarter // 2,
+                pl.ds(quarter % 2 * deep, deep),
+            ],
+            slots.at[quarter],
+            sem_slot.at[quarter],
+        )
+
+    def pair_step(u):
+        first = lax.rem(u, z.pairs) * z.pair
+        sequence_transform([first + q for q in range(z.pair)], u >= z.pairs)
+
+    def single_step(u):
+        sequence_transform([lax.rem(u, groups)], u >= groups)
+
+    def sequence_transform(members, returning):
+        seqs = len(members) * z.group
+
+        for q, g in enumerate(members):
+            wait_all(recv_a.at[g], sem_a.at[g])
+
+            @pl.when(me == 0)
+            def _(g=g):
+                wait_all(recv_sa.at[g], sem_sa.at[g])
+
+            def gather_rows(c, carry, q=q, g=g):
+                columns = pl.ds(pl.multiple_of(c * LANES, LANES), LANES)
+                for parity in range(2):
+                    for s in range(z.group):
+                        at = parity * (z.group // z.pack) + s // z.pack
+                        rows = recv_a[g, c, :, at * LANES : (at + 1) * LANES]
+                        line = recv_sa[g, c, at : at + 1, :]
+                        line = jnp.broadcast_to(line, (16, LANES)).astype(BF16)
+                        if z.pack > 1:
+                            lane = lax.broadcasted_iota(jnp.int32, (per, LANES), 1) // z.half
+                            rows = jnp.where(lane == s % z.pack, rows.astype(F32), 0.0).astype(BF16)
+                            lane = lax.broadcasted_iota(jnp.int32, (16, LANES), 1) // z.half
+                            line = jnp.where(lane == s % z.pack, line.astype(F32), 0.0).astype(BF16)
+                        base = (parity * seqs + q * z.group + s) * z.rows
+                        lhs[base : base + per, columns] = rows
+                        lhs[base + z.per_pad : base + z.rows, columns] = line
+                return carry
+
+            lax.fori_loop(0, parts, gather_rows, 0)
+            wait_sent(g)
+
+            @pl.when((me == 0) & returning)
+            def _(g=g):
+                some = send_sb.at[g, pl.ds(0, parts - 1)]
+                pltpu.make_async_copy(some, some, sem_ssb.at[g]).wait()
+
+        def push_both(g, peer):
+            push(g, peer, recv_b, sem_b)
+
+            @pl.when((me == 0) & (peer != 0))
+            def _():
+                pltpu.make_async_remote_copy(
+                    src_ref=send_sb.at[g, peer],
+                    dst_ref=recv_sb.at[g],
+                    send_sem=sem_ssb.at[g],
+                    recv_sem=sem_sb.at[g],
+                    device_id=(peer, core),
+                    device_id_type=MESH,
+                ).start()
+
+            @pl.when((me == 0) & (peer == 0))
+            def _():
+                pltpu.make_async_copy(send_sb.at[g, 0], recv_sb.at[g], sem_sb.at[g]).start()
+
+        def body(j, carry):
+            near = lax.rem(me + j, half_parts)
+            halves = []
             for parity in range(2):
-                for s in range(z.group):
-                    at = parity * (z.group // z.pack) + s // z.pack
-                    rows = recv_a[g, c, :, at * LANES : (at + 1) * LANES]
-                    line = jnp.broadcast_to(recv_sa[g, c, at : at + 1, :], (16, LANES)).astype(BF16)
-                    if z.pack > 1:
-                        lane = lax.broadcasted_iota(jnp.int32, (per, LANES), 1) // z.half
-                        rows = jnp.where(lane == s % z.pack, rows.astype(F32), 0.0).astype(BF16)
-                        lane = lax.broadcasted_iota(jnp.int32, (16, LANES), 1) // z.half
-                        line = jnp.where(lane == s % z.pack, line.astype(F32), 0.0).astype(BF16)
-                    lhs[parity, s, 0:per, columns] = rows
-                    lhs[parity, s, z.per_pad : z.rows, columns] = line
+                total = 0.0
+                for quarter in (2 * parity, 2 * parity + 1):
+                    fetch(j, quarter).wait()
+                    lanes = slice(quarter % 2 * deep, (quarter % 2 + 1) * deep)
+                    rows = lhs[parity * seqs * z.rows : (parity + 1) * seqs * z.rows, lanes]
+                    total = total + dot(rows, slots[quarter])
+
+                    fetch(j + 1, quarter).start()
+
+                halves.append(total.reshape(seqs, z.rows, z.local))
+
+            even, odd = halves
+            for peer, value in ((near, even + odd), (near + half_parts, even - odd)):
+                for q, g in enumerate(members):
+                    for s in range(z.group):
+                        part = value[q * z.group + s]
+                        lanes = slice(s * z.local, (s + 1) * z.local)
+                        send[g, peer, :, lanes] = part[:per].astype(BF16)
+                        for r in range(z.local // LANES):
+                            at = s * (z.local // LANES) + r
+                            send_sb[g, peer, at : at + 1, :] = part[
+                                z.per_pad : z.per_pad + 1, r * LANES : (r + 1) * LANES
+                            ]
+                push_both(members[0], peer)
             return carry
 
-        lax.fori_loop(0, parts, gather_rows, 0)
-        wait_sent(g)
-
-        @pl.when((me == 0) & (u >= groups))
-        def _():
-            some = send_sb.at[g, pl.ds(0, parts - 1)]
-            pltpu.make_async_copy(some, some, sem_ssb.at[g]).wait()
-
-        def body(j, carry):
-            @pl.when(j + 1 < half_parts)
-            def _():
-                fetch(j + 1).start()
-
-            fetch(j).wait()
-            slot = lax.rem(j, 2)
-            near = lax.rem(me + j, half_parts)
-            even = dot(lhs[0].reshape(z.group * z.rows, z.depth), slots[slot, 0])
-            odd = dot(lhs[1].reshape(z.group * z.rows, z.depth), slots[slot, 1])
-            for peer, value in ((near, even + odd), (near + half_parts, even - odd)):
-                value = value.reshape(z.group, z.rows, z.local)
-                for s in range(z.group):
-                    lanes = slice(s * z.local, (s + 1) * z.local)
-                    send[g, peer, :, lanes] = value[s, :per].astype(BF16)
-                    for r in range(z.local // LANES):
-                        at = s * (z.local // LANES) + r
-                        send_sb[g, peer, at : at + 1, :] = value[
-                            s, z.per_pad : z.per_pad + 1, r * LANES : (r + 1) * LANES
-                        ]
-                push(g, peer, recv_b, sem_b)
-
-                @pl.when((me == 0) & (peer != 0))
-                def _(peer=peer):
-                    pltpu.make_async_remote_copy(
-                        src_ref=send_sb.at[g, peer],
-                        dst_ref=recv_sb.at[g],
-                        send_sem=sem_ssb.at[g],
-                        recv_sem=sem_sb.at[g],
-                        device_id=(peer, core),
-                        device_id_type=MESH,
-                    ).start()
-
-                @pl.when((me == 0) & (peer == 0))
-                def _():
-                    pltpu.make_async_copy(send_sb.at[g, 0], recv_sb.at[g], sem_sb.at[g]).start()
-
-            return carry
-
         lax.fori_loop(0, half_parts, body, 0)
-
-    def mixed_block(g, t):
-        lanes = pl.ds(pl.multiple_of(t * BLOCK, BLOCK), BLOCK)
-        rows = recv_b[g, :, :, lanes]
-        if per % 16:
-            rows = rows.astype(F32).reshape(z.width, BLOCK).astype(BF16)
-        else:
-            rows = rows.reshape(z.width, BLOCK)
-        line = jnp.concatenate(
-            [recv_sb[g, pl.ds(t * (BLOCK // LANES) + r, 1), :] for r in range(BLOCK // LANES)], axis=1
-        )
-        line = jnp.broadcast_to(line, (16, BLOCK)).astype(BF16)
-        return dot_tn(rows, joined[: z.width]) + dot_tn(line, joined[z.width :])
-
-    def mixed_wait(g):
+        for g in members[1:]:
+
+            def later(d, carry, g=g):
+                push_both(g, lax.rem(me + d, parts))
+                return carry
+
+            lax.fori_loop(0, parts, later, 0)
+
+    def mixed(g):
         wait_all(recv_b.at[g], sem_b.at[g])
         wait_all(recv_sb.at[g], sem_sb.at[g])
+        rows = recv_b[g]
+        if per % 16:
+            rows = rows.astype(F32).reshape(z.width, z.glen).astype(BF16)
+        else:
+            rows = rows.reshape(z.width, z.glen)
+        line = jnp.concatenate([recv_sb[g, r : r + 1, :] for r in range(z.glen // LANES)], axis=1)
+        line = jnp.broadcast_to(line, (16, z.glen)).astype(BF16)
+        return dot_tn(rows, joined[: z.width]) + dot_tn(line, joined[z.width :])
+
+    def tokens_of(g):
+        return pl.ds(pl.multiple_of(g * z.glen, z.glen), z.glen)
 
     def feed_step(g):
-        tokens = pl.ds(pl.multiple_of(g * z.glen, z.glen), z.glen)
-        load_x = pltpu.make_async_copy(x_hbm.at[tokens], xs, sem_local.at[4])
-        load_c = pltpu.make_async_copy(cot_hbm.at[tokens], cs, sem_local.at[5])
+        load_x = pltpu.make_async_copy(x_hbm.at[tokens_of(g)], source, sem_local.at[4])
+        load_c = pltpu.make_async_copy(cot_hbm.at[tokens_of(g)], cs, sem_local.at[5])
+        put_result = pltpu.make_async_copy(stage, result_hbm.at[tokens_of(g)], sem_local.at[6])
+        put_grad = pltpu.make_async_copy(work, grad_hbm.at[tokens_of(g)], sem_local.at[7])
         load_x.start()
         load_c.start()
-        mixed_wait(g)
+        value = mixed(g)
         load_x.wait()
         load_c.wait()
-
-        def block(t, carry):
-            rows = pl.ds(pl.multiple_of(t * BLOCK, BLOCK), BLOCK)
-            outer = pl.ds(pl.multiple_of(g * z.glen + t * BLOCK, BLOCK), BLOCK)
-            value = xs[rows, :].astype(F32) + mixed_block(g, t)
-            normed, inverse = normalize(value)
-            normed_one[...] = normed
-            inverse_one[...] = inverse
-            value = normed * vectors[0:1, :] + vectors[1:2, :]
-            hidden[...] = value
-            low[...] = value.astype(BF16)
-            work[...] = jnp.zeros_like(work)
-
-            def forward(c, carry):
-                lanes = pl.ds(pl.multiple_of(c * z.width, z.width), z.width)
-                some = pl.ds(c * z.chunk_shards, z.chunk_shards)
-                pre = dot_nt(low[...], full_in[some].reshape(z.width, z.width)) + bias[:, lanes]
-                value, pull = gelu_and_slope(pre)
-                value = value.astype(BF16)
-                act[:, lanes] = value
-                slope[:, lanes] = pull.astype(BF16)
-                work[...] += dot(value, full_out[some].reshape(z.width, z.width))
-                return carry
-
-            lax.fori_loop(0, z.chunks, forward, 0)
-            normed, inverse = normalize(hidden[...] + (work[...] + vectors[4:5, :]))
-            stage[...] = normed * vectors[2:3, :] + vectors[3:4, :]
-            put = pltpu.make_async_copy(stage, result_hbm.at[outer], sem_local.at[6])
-            put.start()
-            grad = cs[rows, :].astype(F32)
-            here = pl.ds(z.hidden, z.width)
-            vec_sum[2:3, here] += jnp.sum(grad * normed, axis=0, keepdims=True)
-            vec_sum[3:4, here] += jnp.sum(grad, axis=0, keepdims=True)
-            grad = norm_backward(grad * vectors[2:3, :], normed, inverse)
-            work[...] = grad
-            dffo = grad.astype(BF16)
-            dlow[...] = dffo
-            vec_sum[4:5, here] += jnp.sum(dffo.astype(F32), axis=0, keepdims=True)
-
-            def backward(c, carry):
-                lanes = pl.ds(pl.multiple_of(c * z.width, z.width), z.width)
-                some = pl.ds(c * z.chunk_shards, z.chunk_shards)
-                shape = (z.chunk_shards, z.shard_rows, z.width)
-                dpre = dot_nt(dlow[...], full_out[some].reshape(z.width, z.width))
-                dpre = (dpre * slope[:, lanes].astype(F32)).astype(BF16)
-                vec_sum[0:1, lanes] += jnp.sum(dpre.astype(F32), axis=0, keepdims=True)
-                work[...] += dot(dpre, full_in[some].reshape(z.width, z.width))
-                into_out = dot_tn(act[:, lanes], dlow[...]).reshape(shape)
-                into_in = dot_tn(dpre, low[...]).reshape(shape)
-
-                @pl.when(g + t == 0)
-                def _():
-                    sum_out[some] = into_out
-                    sum_in[some] = into_in
-
-                @pl.when(g + t > 0)
-                def _():
-                    sum_out[some] += into_out
-                    sum_in[some] += into_in
-
-                return carry
-
-            lax.fori_loop(0, z.chunks, backward, 0)
-            grad, normed = work[...], normed_one[...]
-            vec_sum[0:1, here] += jnp.sum(grad * normed, axis=0, keepdims=True)
-            vec_sum[1:2, here] += jnp.sum(grad, axis=0, keepdims=True)
-            grad = norm_backward(grad * vectors[0:1, :], normed, inverse_one[...])
-            source[rows, :] = grad.astype(BF16)
-            put.wait()
-            stage[...] = grad
-            put = pltpu.make_async_copy(stage, grad_hbm.at[outer], sem_local.at[6])
-            put.start()
-            put.wait()
+        normed, inverse = normalize(source[...].astype(F32) + value)
+        normed_one[...] = normed
+        inverse_one[...] = inverse
+        low[...] = (normed * vectors[0:1, :] + vectors[1:2, :]).astype(BF16)
+        work[...] = jnp.zeros_like(work)
+
+        def forward(c, carry):
+            lanes = pl.ds(pl.multiple_of(c * z.width, z.width), z.width)
+            some = pl.ds(c * z.chunk_shards, z.chunk_shards)
+            pre = dot_nt(low[...], full_in[some].reshape(z.width, z.width)) + bias[:, lanes]
+            value, pull = gelu_and_slope(pre)
+            value = value.astype(BF16)
+            act[:, lanes] = value
+            slope[:, lanes] = pull.astype(BF16)
+            work[...] += dot(value, full_out[some].reshape(z.width, z.width))
             return carry
 
-        lax.fori_loop(0, z.blocks, block, 0)
+        lax.fori_loop(0, z.chunks, forward, 0, unroll=2)
+        value = normed_one[...] * vectors[0:1, :] + vectors[1:2, :]
+        normed, inverse = normalize(value + (work[...] + vectors[4:5, :]))
+        stage[...] = normed * vectors[2:3, :] + vectors[3:4, :]
+        put_result.start()
+        grad = cs[...].astype(F32)
+        here = pl.ds(z.hidden, z.width)
+        vec_sum[2:3, here] += jnp.sum(grad * normed, axis=0, keepdims=True)
+        vec_sum[3:4, here] += jnp.sum(grad, axis=0, keepdims=True)
+        grad = norm_backward(grad * vectors[2:3, :], normed, inverse)
+        work[...] = grad
+        dffo = grad.astype(BF16)
+        dlow[...] = dffo
+        vec_sum[4:5, here] += jnp.sum(dffo.astype(F32), axis=0, keepdims=True)
+
+        def backward(c, carry):
+            lanes = pl.ds(pl.multiple_of(c * z.width, z.width), z.width)
+            some = pl.ds(c * z.chunk_shards, z.chunk_shards)
+            shape = (z.chunk_shards, z.shard_rows, z.width)
+            dpre = dot_nt(dlow[...], full_out[some].reshape(z.width, z.width))
+            dpre = (dpre * slope[:, lanes].astype(F32)).astype(BF16)
+            vec_sum[0:1, lanes] += jnp.sum(dpre.astype(F32), axis=0, keepdims=True)
+            work[...] += dot(dpre, full_in[some].reshape(z.width, z.width))
+            into_out = dot_tn(act[:, lanes], dlow[...]).reshape(shape)
+            into_in = dot_tn(dpre, low[...]).reshape(shape)
+
+            @pl.when(g == 0)
+            def _():
+                sum_out[some] = into_out
+                sum_in[some] = into_in
+
+            @pl.when(g > 0)
+            def _():
+                sum_out[some] += into_out
+                sum_in[some] += into_in
+
+            return carry
+
+        lax.fori_loop(0, z.chunks, backward, 0)
+        grad, normed = work[...], normed_one[...]
+        vec_sum[0:1, here] += jnp.sum(grad * normed, axis=0, keepdims=True)
+        vec_sum[1:2, here] += jnp.sum(grad, axis=0, keepdims=True)
+        grad = norm_backward(grad * vectors[0:1, :], normed, inverse_one[...])
+        source[...] = grad.astype(BF16)
+        work[...] = grad
+        put_grad.start()
         hidden_step(g + groups)
+        put_result.wait()
+        put_grad.wait()
+
+    def finish_put(g):
+        return pltpu.make_async_copy(stage, grad_hbm.at[tokens_of(g)], sem_local.at[6])
 
     def finish_step(g):
-        def load(t):
-            outer = pl.ds(pl.multiple_of(g * z.glen + t * BLOCK, BLOCK), BLOCK)
-            return pltpu.make_async_copy(grad_hbm.at[outer], work, sem_local.at[7])
-
-        load(0).start()
-        mixed_wait(g)
-
-        def block(t, carry):
-            outer = pl.ds(pl.multiple_of(g * z.glen + t * BLOCK, BLOCK), BLOCK)
-
-            @pl.when(t > 0)
-            def _():
-                load(t).start()
-
-            value = mixed_block(g, t)
-            load(t).wait()
-            stage[...] = work[...] + value
-            put = pltpu.make_async_copy(stage, grad_hbm.at[outer], sem_local.at[6])
-            put.start()
-            put.wait()
-            return carry
-
-        lax.fori_loop(0, z.blocks, block, 0)
+        load = pltpu.make_async_copy(grad_hbm.at[tokens_of(g)], work, sem_local.at[7])
+        load.start()
+        value = mixed(g)
+        load.wait()
+
+        @pl.when(g > 0)
+        def _():
+            finish_put(g - 1).wait()
+
+        stage[...] = work[...] + value
+        finish_put(g).start()
 
     offsets = [sum(1 << (z.bits - 1 - i) for i in range(s)) for s in range(z.bits)]
 
@@ -731,7 +724,16 @@
                     scatter_send(s)
 
     steps = plan(z)
-    bodies = (hidden_step, gather_step, seqmix_step, feed_step, scatter_step, finish_step)
+    bodies = (
+        hidden_step,
+        gather_step,
+        pair_step,
+        single_step,
+        feed_step,
+        scatter_step,
+        finish_step,
+    )
+    used = {name for name, _ in steps}
 
     def one_step(s, carry):
         kind, argument = 0, 0
@@ -740,6 +742,8 @@
             kind = kind + here * KINDS.index(name)
             argument = argument + here * value
         for k, body in enumerate(bodies):
+            if KINDS[k] not in used:
+                continue
 
             @pl.when(kind == k)
             def _(body=body):
@@ -747,11 +751,16 @@
 
         return carry
 
+    for quarter in range(4):
+        fetch(0, quarter).start()
     lax.fori_loop(0, len(steps), one_step, 0)
+    for quarter in range(4):
+        fetch(0, quarter).wait()
 
     for w, total in ((0, total_in), (1, total_out)):
         pltpu.make_async_copy(sums[w].at[mine], total, sem_local.at[w]).start()
     pltpu.make_async_copy(vec_sum, total_vec, sem_local.at[2]).start()
+    finish_put(groups - 1).wait()
     for g in range(groups):
         wait_sent(g)
 
@@ -777,7 +786,7 @@
     tokens = z.seqs * z.local
     vec_lanes = z.hidden + z.width
     shard = (z.shards, z.shard_rows, z.width)
-    block = (BLOCK, z.width)
+    block = (z.glen, z.width)
     any_space, vmem = pl.BlockSpec(memory_space=pl.ANY), pl.BlockSpec(memory_space=pltpu.VMEM)
     dma = pltpu.SemaphoreType.DMA
     g = z.groups
@@ -798,20 +807,18 @@
         pltpu.VMEM((g, 8, LANES), F32),
         pltpu.VMEM((g, 8, LANES), F32),
         pltpu.VMEM((g, z.parts, 8, LANES), F32),
-        pltpu.VMEM((2, z.group, z.rows, z.depth), BF16),
-        pltpu.VMEM((2, 2, z.depth, z.local), BF16),
+        pltpu.VMEM((16, LANES) if z.shared else (z.lhs_rows, z.depth), BF16),
+        pltpu.VMEM((4, z.depth // 2, z.local), BF16),
         pltpu.VMEM((z.glen, z.width), BF16),
         pltpu.VMEM((z.glen, z.width), BF16),
-        pltpu.VMEM((z.glen, z.width), BF16),
-        pltpu.VMEM((BLOCK, z.hidden), BF16),
-        pltpu.VMEM((BLOCK, z.hidden), BF16),
-        pltpu.VMEM(block, F32),
+        pltpu.VMEM((z.glen, z.hidden), BF16),
+        pltpu.VMEM((z.glen, z.hidden), BF16),
         pltpu.VMEM(block, F32),
         pltpu.VMEM(block, BF16),
         pltpu.VMEM(block, BF16),
         pltpu.VMEM(block, F32),
         pltpu.VMEM(block, F32),
-        pltpu.VMEM((BLOCK, 1), F32),
+        pltpu.VMEM((z.glen, 1), F32),
         dma((g,)),
         dma((g,)),
         dma((g,)),
@@ -824,7 +831,7 @@
         dma((3, z.bits)),
         dma((3, z.bits)),
         dma((8,)),
-        dma((2,)),
+        dma((4,)),
     ]
     return pl.pallas_call(
         functools.partial(step_kernel, z),

time: 434 us -> 396 us (0.912)
  Pallas kernels: 410 us -> 373 us
    pallas_call x1, Pallas kernels: 410 us -> 373 us  [run_step(): pl.pallas_call(functools.partial(step_kernel, z), out_shape=(jax.ShapeDty...]
where the time goes in v2:
time: 396 us; the launch traced here: 395 us
  Pallas kernels  373 us (94%)
  other arithmetic  11.9 us (3%)
  local copies, waits for them, and re-layouts  9.72 us (2%)
    pallas_call x1, Pallas kernels, run_step(): pl.pallas_call(functools.partial(step_kernel, z), out_shape=(jax.ShapeDty...  373 us
    unnamed x6, local copies, waits for them, and re-layouts  8.81 us

profile of v2, /device:TPU:24, one launch (start us, length us, event | category | flops | bytes accessed | tf_op | source)
XLA Modules:
  0.0 395.1 jit_solution(13621987592090372041)
XLA Ops:
  0.6 1.6 convert_bitcast_fusion.shard_in
  2.3 1.6 convert_element_type.14.shard_out
  3.9 1.3 select_maximum_fusion.shard_vec
  5.2 372.8 %shard_map.281 = (f32[2048,768]{1,0:T(8,128)}, f32[2048,768]{1,0:T(8,128)}, f32[96,768]{1,0:T(8,128)}, f32[96,768]{1,0:T(8,128)}, f32[8,3840]{1,0:T(8,128)}, /*index=5*/bf16[2,31,96,768]{3,2,1,0:T(8,128)(2,1)}) custom-call(bf16[2048,768]{1,0:T(8,128)(2,1)} %bitcast.32, bf16[2048,768]{1,0:T(8,128)(2,1)} %bitcast.33, ...), custom_call_target="tpu_custom_call" | custom-call | flops 64424509440 | bytes 62914560 | tf_op jit(solution)/shard_map/pallas_call | solution.py:836
  378.1 2.2 multiply_add_fusion.2
  380.3 0.0 slice-start
  380.3 2.4 multiply_add_fusion
  382.7 0.9 slice.6
  383.6 1.3 multiply_add_fusion.5
  384.8 1.4 multiply_add_fusion.3
  386.3 0.0 slice-start.1
  386.3 6.1 %copy.34 = f32[8,256,768]{2,1,0:T(8,128)} copy(f32[8,256,768]{2,1,0:T(8,128)} %bitcast.29) | data formatting | bytes 12582912
  392.4 0.0 slice-done
  392.4 0.0 slice-done.1
  392.4 2.7 copy.35
  (1 shorter events, 0.0 us)
Async XLA Ops:
  380.3 12.1 %slice-start = ((s8[6291456]{0:T(1024)(128)(4,1)}), s8[2097152]{0:T(1024)(128)(4,1)S(1)}, s32[]{:S(2)}) async-start(s8[6291456]{0:T(1024)(128)(4,1)} %bitcast.26), calls=%async_computation | async-start | bytes 4194304
  386.3 6.1 %slice-start.1 = ((s8[6291456]{0:T(1024)(128)(4,1)}), s8[4194304]{0:T(1024)(128)(4,1)S(1)}, s32[]{:S(2)}) async-start(s8[6291456]{0:T(1024)(128)(4,1)} %bitcast.26), calls=%async_computation.1 | async-start | bytes 8388608

commit v3 on v2

--- a/solution.py
+++ b/solution.py
@@ -50,8 +50,10 @@
         self.shard_rows = hidden // self.shards
         self.chunks = hidden // width
         self.chunk_shards = self.shards // self.chunks
+        self.pieces = 3
+        assert self.chunks <= 8 and self.shard_rows % (16 * self.pieces) == 0
         assert parts == 1 << self.seq_bits and self.half * self.pack == LANES
-        assert self.group % self.pack == 0 and self.shard_rows % 16 == 0
+        assert self.group % self.pack == 0
 
 
 def mixing_tables(z):
@@ -155,9 +157,9 @@
 
 
 ORDER = (
-    "G1", "H0", "G2", "H1", "G3", "H2", "H3", "T0", "G4", "T1", "G5",
-    "F0", "F1", "F2", "T2", "F3", "S0", "t6", "S1", "S2", "t7", "E0",
-    "S3", "E1", "E2", "S4", "E3", "S5",
+    "G1", "H0", "G2", "H1", "G3", "t0", "H2", "H3", "G4", "t1", "G5",
+    "F0", "T1", "F1", "F2", "T2", "F3", "S0", "t6", "S1", "S2", "t7",
+    "E0", "S3", "E1", "E2", "S4", "E3", "S5",
 )
 
 
@@ -189,11 +191,9 @@
     total_out,
     total_vec,
     landed,
-    full_in,
-    full_out,
+    full,
     full_vec,
-    sum_in,
-    sum_out,
+    sums,
     bias,
     vectors,
     vec_sum,
@@ -234,18 +234,17 @@
     parts, per, groups = z.parts, z.per, z.groups
     me = lax.axis_index("seq")
     core = lax.axis_index("batch")
-    fulls = (full_in, full_out, full_vec)
-    sums = (sum_in, sum_out)
     lhs = act if z.shared else own_lhs
 
     own = [lax.rem(lax.div(me, 1 << (z.seq_bits - 1 - d)), 2) for d in range(z.seq_bits)]
     own += [core] if z.with_batch else []
     weights = [1 << (z.bits - 1 - d) for d in range(z.bits)]
-    first = list(range(z.bits))
-    second = list(first)
-    a, b = z.seq_bits - 2, z.seq_bits - 1
-    second[a], second[b] = second[b], second[a]
-    gather_orders = (first, second, first)
+    middle = list(range(1, z.bits - 1))
+    orders = [[0] + middle[r:] + middle[:r] + [z.bits - 1] for r in range(z.pieces)]
+    piece_rows = z.shard_rows // z.pieces
+
+    def piece(at, w):
+        return full.at[:, at, pl.ds(w * piece_rows, piece_rows)]
 
     def partner(d):
         if d < z.seq_bits:
@@ -278,8 +277,14 @@
     greeted = parts - 1 + (1 if z.with_batch else 0)
 
     mine = shard_at((), 0)
-    for w, shard in enumerate((shard_in, shard_out, shard_vec)):
-        pltpu.make_async_copy(shard, fulls[w].at[mine], sem_local.at[w]).start()
+    own_shards = [
+        pltpu.make_async_copy(shard, place.at[mine], sem_local.at[w])
+        for w, (shard, place) in enumerate(
+            ((shard_in, full.at[0]), (shard_out, full.at[1]), (shard_vec, full_vec))
+        )
+    ]
+    for copy in own_shards:
+        copy.start()
     send_sa[...] = jnp.zeros_like(send_sa)
     vec_sum[...] = jnp.zeros_like(vec_sum)
 
@@ -290,15 +295,16 @@
     pl.semaphore_wait(barrier, greeted)
 
     def gather_send(stage_no):
-        for w in range(3):
-            order_w = gather_orders[w]
-            free, d = order_w[:stage_no], order_w[stage_no]
+        for w in range(z.pieces + 1):
+            path = orders[w % z.pieces]
+            free, d = path[:stage_no], path[stage_no]
 
             def body(k, carry, w=w, free=free, d=d):
                 at = shard_at(free, k)
+                block = piece(at, w) if w < z.pieces else full_vec.at[at]
                 pltpu.make_async_remote_copy(
-                    src_ref=fulls[w].at[at],
-                    dst_ref=fulls[w].at[at],
+                    src_ref=block,
+                    dst_ref=block,
                     send_sem=sem_gather_send.at[w, stage_no],
                     recv_sem=sem_gather_recv.at[w, stage_no],
                     device_id=partner(d),
@@ -308,19 +314,24 @@
 
             lax.fori_loop(0, 1 << stage_no, body, 0)
 
+    def gather_some(w, stage_no):
+        if w < z.pieces:
+            return landed.at[w, pl.ds(0, 1 << stage_no)]
+        return full_vec.at[pl.ds(0, 1 << stage_no)]
+
     def gather_wait(stage_no):
-        for w in range(3):
-            some = fulls[w].at[pl.ds(0, 1 << stage_no)]
+        for w in range(z.pieces + 1):
+            some = gather_some(w, stage_no)
             pltpu.make_async_copy(some, some, sem_gather_recv.at[w, stage_no]).wait()
 
     def gather_done():
         for stage_no in range(z.bits):
-            for w in range(3):
-                some = fulls[w].at[pl.ds(0, 1 << stage_no)]
+            for w in range(z.pieces + 1):
+                some = gather_some(w, stage_no)
                 pltpu.make_async_copy(some, some, sem_gather_send.at[w, stage_no]).wait()
 
-    for w, shard in enumerate((shard_in, shard_out, shard_vec)):
-        pltpu.make_async_copy(shard, fulls[w].at[mine], sem_local.at[w]).wait()
+    for copy in own_shards:
+        copy.wait()
     gather_send(0)
 
     def gather_step(i):
@@ -573,12 +584,12 @@
         def forward(c, carry):
             lanes = pl.ds(pl.multiple_of(c * z.width, z.width), z.width)
             some = pl.ds(c * z.chunk_shards, z.chunk_shards)
-            pre = dot_nt(low[...], full_in[some].reshape(z.width, z.width)) + bias[:, lanes]
+            pre = dot_nt(low[...], full[0, some].reshape(z.width, z.width)) + bias[:, lanes]
             value, pull = gelu_and_slope(pre)
             value = value.astype(BF16)
             act[:, lanes] = value
             slope[:, lanes] = pull.astype(BF16)
-            work[...] += dot(value, full_out[some].reshape(z.width, z.width))
+            work[...] += dot(value, full[1, some].reshape(z.width, z.width))
             return carry
 
         lax.fori_loop(0, z.chunks, forward, 0, unroll=2)
@@ -587,42 +598,41 @@
         stage[...] = normed * vectors[2:3, :] + vectors[3:4, :]
         put_result.start()
         grad = cs[...].astype(F32)
-        here = pl.ds(z.hidden, z.width)
-        vec_sum[2:3, here] += jnp.sum(grad * normed, axis=0, keepdims=True)
-        vec_sum[3:4, here] += jnp.sum(grad, axis=0, keepdims=True)
+        vec_sum[10:11, :] += jnp.sum(grad * normed, axis=0, keepdims=True)
+        vec_sum[11:12, :] += jnp.sum(grad, axis=0, keepdims=True)
         grad = norm_backward(grad * vectors[2:3, :], normed, inverse)
         work[...] = grad
         dffo = grad.astype(BF16)
         dlow[...] = dffo
-        vec_sum[4:5, here] += jnp.sum(dffo.astype(F32), axis=0, keepdims=True)
+        vec_sum[12:13, :] += jnp.sum(dffo.astype(F32), axis=0, keepdims=True)
 
         def backward(c, carry):
             lanes = pl.ds(pl.multiple_of(c * z.width, z.width), z.width)
             some = pl.ds(c * z.chunk_shards, z.chunk_shards)
             shape = (z.chunk_shards, z.shard_rows, z.width)
-            dpre = dot_nt(dlow[...], full_out[some].reshape(z.width, z.width))
+            dpre = dot_nt(dlow[...], full[1, some].reshape(z.width, z.width))
             dpre = (dpre * slope[:, lanes].astype(F32)).astype(BF16)
-            vec_sum[0:1, lanes] += jnp.sum(dpre.astype(F32), axis=0, keepdims=True)
-            work[...] += dot(dpre, full_in[some].reshape(z.width, z.width))
+            vec_sum[pl.ds(c, 1), :] += jnp.sum(dpre.astype(F32), axis=0, keepdims=True)
+            work[...] += dot(dpre, full[0, some].reshape(z.width, z.width))
             into_out = dot_tn(act[:, lanes], dlow[...]).reshape(shape)
             into_in = dot_tn(dpre, low[...]).reshape(shape)
 
             @pl.when(g == 0)
             def _():
-                sum_out[some] = into_out
-                sum_in[some] = into_in
+                sums[1, some] = into_out
+                sums[0, some] = into_in
 
             @pl.when(g > 0)
             def _():
-                sum_out[some] += into_out
-                sum_in[some] += into_in
+                sums[1, some] += into_out
+                sums[0, some] += into_in
 
             return carry
 
         lax.fori_loop(0, z.chunks, backward, 0)
         grad, normed = work[...], normed_one[...]
-        vec_sum[0:1, here] += jnp.sum(grad * normed, axis=0, keepdims=True)
-        vec_sum[1:2, here] += jnp.sum(grad, axis=0, keepdims=True)
+        vec_sum[8:9, :] += jnp.sum(grad * normed, axis=0, keepdims=True)
+        vec_sum[9:10, :] += jnp.sum(grad, axis=0, keepdims=True)
         grad = norm_backward(grad * vectors[0:1, :], normed, inverse_one[...])
         source[...] = grad.astype(BF16)
         work[...] = grad
@@ -649,22 +659,18 @@
 
     offsets = [sum(1 << (z.bits - 1 - i) for i in range(s)) for s in range(z.bits)]
 
-    def scatter_orders(w):
-        if w < 2:
-            return gather_orders[w][::-1]
-        return gather_orders[0][::-1]
-
     def scatter_send(s):
         count = 1 << (z.bits - 1 - s)
-        for w in range(2):
-            path = scatter_orders(w)
+        for w in range(z.pieces):
+            path = orders[w][::-1]
             d, free = path[s], path[s + 1 :]
 
             def body(k, carry, w=w, d=d, free=free):
                 at = shard_at(free, k, flipped=d)
-                fulls[w][at] = sums[w][at].astype(BF16)
+                rows = pl.ds(w * piece_rows, piece_rows)
+                full[:, at, rows] = sums[:, at, rows].astype(BF16)
                 pltpu.make_async_remote_copy(
-                    src_ref=fulls[w].at[at],
+                    src_ref=piece(at, w),
                     dst_ref=landed.at[w, offsets[s] + k],
                     send_sem=sem_scatter_send.at[w, s],
                     recv_sem=sem_scatter_recv.at[w, s],
@@ -677,38 +683,37 @@
         pltpu.make_async_remote_copy(
             src_ref=vec_sum,
             dst_ref=vec_land.at[s],
-            send_sem=sem_scatter_send.at[2, s],
-            recv_sem=sem_scatter_recv.at[2, s],
-            device_id=partner(scatter_orders(2)[s]),
+            send_sem=sem_scatter_send.at[z.pieces, s],
+            recv_sem=sem_scatter_recv.at[z.pieces, s],
+            device_id=partner(orders[0][::-1][s]),
             device_id_type=MESH,
         ).start()
 
     def scatter_add(s):
         count = 1 << (z.bits - 1 - s)
-        for w in range(2):
-            path = scatter_orders(w)
-            free = path[s + 1 :]
+        for w in range(z.pieces):
+            free = orders[w][::-1][s + 1 :]
             some = landed.at[w, pl.ds(offsets[s], count)]
             wait_all(some, sem_scatter_recv.at[w, s])
 
             def fetch(k, carry, w=w, free=free):
                 pltpu.make_async_copy(
-                    landed.at[w, offsets[s] + k], fulls[w].at[shard_at(free, k)], sem_local.at[w]
+                    landed.at[w, offsets[s] + k], piece(shard_at(free, k), w), sem_local.at[w]
                 ).start()
                 return carry
 
             lax.fori_loop(0, count, fetch, 0)
-        wait_all(vec_sum, sem_scatter_send.at[2, s])
-        wait_all(vec_land.at[s], sem_scatter_recv.at[2, s])
+        wait_all(vec_sum, sem_scatter_send.at[z.pieces, s])
+        wait_all(vec_land.at[s], sem_scatter_recv.at[z.pieces, s])
         vec_sum[...] += vec_land[s]
-        for w in range(2):
-            free = scatter_orders(w)[s + 1 :]
+        for w in range(z.pieces):
+            free = orders[w][::-1][s + 1 :]
             some = landed.at[w, pl.ds(offsets[s], count)]
             wait_all(some, sem_local.at[w])
 
             def add(k, carry, w=w, free=free):
-                at = shard_at(free, k)
-                sums[w][at] += fulls[w][at].astype(F32)
+                at, rows = shard_at(free, k), pl.ds(w * piece_rows, piece_rows)
+                sums[:, at, rows] += full[:, at, rows].astype(F32)
                 return carry
 
             lax.fori_loop(0, count, add, 0)
@@ -758,7 +763,7 @@
         fetch(0, quarter).wait()
 
     for w, total in ((0, total_in), (1, total_out)):
-        pltpu.make_async_copy(sums[w].at[mine], total, sem_local.at[w]).start()
+        pltpu.make_async_copy(sums.at[w, mine], total, sem_local.at[w]).start()
     pltpu.make_async_copy(vec_sum, total_vec, sem_local.at[2]).start()
     finish_put(groups - 1).wait()
     for g in range(groups):
@@ -774,32 +779,30 @@
             pltpu.make_async_copy(some, some, sem_ssb.at[g]).wait()
 
     for s in range(z.bits):
-        for w in range(2):
+        for w in range(z.pieces):
             some = landed.at[w, pl.ds(offsets[s], 1 << (z.bits - 1 - s))]
             wait_all(some, sem_scatter_send.at[w, s])
     for w, total in ((0, total_in), (1, total_out)):
-        pltpu.make_async_copy(sums[w].at[mine], total, sem_local.at[w]).wait()
+        pltpu.make_async_copy(sums.at[w, mine], total, sem_local.at[w]).wait()
     pltpu.make_async_copy(vec_sum, total_vec, sem_local.at[2]).wait()
 
 
 def run_step(z, x, cot, shard_in, shard_out, shard_vec, tables):
     tokens = z.seqs * z.local
-    vec_lanes = z.hidden + z.width
-    shard = (z.shards, z.shard_rows, z.width)
+    shard = (2, z.shards, z.shard_rows, z.width)
+    piece = (2, z.shard_rows // z.pieces, z.width)
     block = (z.glen, z.width)
     any_space, vmem = pl.BlockSpec(memory_space=pl.ANY), pl.BlockSpec(memory_space=pltpu.VMEM)
     dma = pltpu.SemaphoreType.DMA
     g = z.groups
     scratch = [
         pltpu.VMEM(shard, BF16),
-        pltpu.VMEM(shard, BF16),
         pltpu.VMEM((z.shards, 16, LANES), F32),
-        pltpu.VMEM(shard, F32),
         pltpu.VMEM(shard, F32),
         pltpu.VMEM((1, z.hidden), F32),
         pltpu.VMEM((8, z.width), F32),
-        pltpu.VMEM((8, vec_lanes), F32),
-        pltpu.VMEM((z.bits, 8, vec_lanes), F32),
+        pltpu.VMEM((16, z.width), F32),
+        pltpu.VMEM((z.bits, 16, z.width), F32),
         pltpu.VMEM((g, z.parts, z.per, z.glen), BF16),
         pltpu.VMEM((g, z.parts, z.per, z.glen), BF16),
         pltpu.VMEM((g, z.parts, z.per, z.glen), BF16),
@@ -826,10 +829,10 @@
         dma((g,)),
         dma((g,)),
         dma((g,)),
-        dma((3, z.bits)),
-        dma((3, z.bits)),
-        dma((3, z.bits)),
-        dma((3, z.bits)),
+        dma((z.pieces + 1, z.bits)),
+        dma((z.pieces + 1, z.bits)),
+        dma((z.pieces + 1, z.bits)),
+        dma((z.pieces + 1, z.bits)),
         dma((8,)),
         dma((4,)),
     ]
@@ -838,10 +841,10 @@
         out_shape=(
             jax.ShapeDtypeStruct((tokens, z.width), F32),
             jax.ShapeDtypeStruct((tokens, z.width), F32),
-            jax.ShapeDtypeStruct(shard[1:], F32),
-            jax.ShapeDtypeStruct(shard[1:], F32),
-            jax.ShapeDtypeStruct((8, vec_lanes), F32),
-            jax.ShapeDtypeStruct((2, z.shards - 1) + shard[1:], BF16),
+            jax.ShapeDtypeStruct(shard[2:], F32),
+            jax.ShapeDtypeStruct(shard[2:], F32),
+            jax.ShapeDtypeStruct((16, z.width), F32),
+            jax.ShapeDtypeStruct((z.pieces, z.shards - 1) + piece, BF16),
         ),
         in_specs=[any_space] * 6 + [vmem] * 3,
         out_specs=(any_space,) * 6,
@@ -917,8 +920,8 @@
         grad_out = lax.psum_scatter(grad_out, "batch", scatter_dimension=0, tiled=True)
         grad_vec = lax.psum(grad_vec, "batch")
     count, narrow = hidden // devices, width // devices
-    grad_bias = lax.dynamic_slice(grad_vec[0], (index * count,), (count,))
-    grad_norm = lax.dynamic_slice(grad_vec[:5], (0, hidden + index * narrow), (5, narrow))
+    grad_bias = lax.dynamic_slice(grad_vec[: z.chunks].reshape(hidden), (index * count,), (count,))
+    grad_norm = lax.dynamic_slice(grad_vec[8:13], (0, index * narrow), (5, narrow))
 
     scale = (seqs * batch_parts * local * seq_parts) ** (-0.5)
     m_in, w_in_new, a_in = nesterov(

time: 396 us -> 364 us (0.919)
  Pallas kernels: 373 us -> 339 us
    pallas_call x1, Pallas kernels: 373 us -> 339 us  [run_step(): pl.pallas_call(functools.partial(step_kernel, z), out_shape=(jax.ShapeDty...]
where the time goes in v3:
time: 364 us; the launch traced here: 362 us
  Pallas kernels  339 us (93%)
  other arithmetic  11.7 us (3%)
  local copies, waits for them, and re-layouts  10.4 us (3%)
    pallas_call x1, Pallas kernels, run_step(): pl.pallas_call(functools.partial(step_kernel, z), out_shape=(jax.ShapeDty...  339 us
    unnamed x6, local copies, waits for them, and re-layouts  8.81 us

profile of v3, /device:TPU:24, one launch (start us, length us, event | category | flops | bytes accessed | tf_op | source)
XLA Modules:
  0.0 361.9 jit_solution(9792961466263484619)
XLA Ops:
  0.6 1.6 convert_bitcast_fusion.shard_in
  2.3 1.6 convert_element_type.14.shard_out
  3.9 1.3 select_maximum_fusion.shard_vec
  5.2 339.0 %shard_map.281 = (f32[2048,768]{1,0:T(8,128)}, f32[2048,768]{1,0:T(8,128)}, f32[96,768]{1,0:T(8,128)}, f32[96,768]{1,0:T(8,128)}, f32[16,768]{1,0:T(8,128)}, /*index=5*/bf16[3,31,2,32,768]{4,3,2,1,0:T(8,128)(2,1)}) custom-call(bf16[2048,768]{1,0:T(8,128)(2,1)} %bitcast.21, bf16[2048,768]{1,0:T(8,128)(2,1)} %bitcast.22, ...), custom_call_target="tpu_custom_call" | custom-call | flops 64424509440 | bytes 62914560 | tf_op jit(solution)/shard_map/pallas_call | solution.py:839
  344.3 2.2 multiply_add_fusion.2
  346.5 2.2 multiply_add_fusion
  348.7 0.0 slice-start
  348.7 0.9 slice.6
  349.6 1.3 multiply_add_fusion.5
  350.9 0.7 slice.7
  351.6 1.4 multiply_add_fusion.3
  353.0 0.0 slice-start.1
  353.0 6.1 %copy.34 = f32[8,256,768]{2,1,0:T(8,128)} copy(f32[8,256,768]{2,1,0:T(8,128)} %bitcast.19) | data formatting | bytes 12582912
  359.1 0.0 slice-done
  359.1 0.0 slice-done.1
  359.1 2.7 copy.35
  (2 shorter events, 0.0 us)
Async XLA Ops:
  348.7 10.4 %slice-start = ((s8[6291456]{0:T(1024)(128)(4,1)}), s8[2097152]{0:T(1024)(128)(4,1)S(1)}, s32[]{:S(2)}) async-start(s8[6291456]{0:T(1024)(128)(4,1)} %bitcast.16), calls=%async_computation | async-start | bytes 4194304
  353.0 6.1 %slice-start.1 = ((s8[6291456]{0:T(1024)(128)(4,1)}), s8[4194304]{0:T(1024)(128)(4,1)S(1)}, s32[]{:S(2)}) async-start(s8[6291456]{0:T(1024)(128)(4,1)} %bitcast.16), calls=%async_computation.1 | async-start | bytes 8388608

commit v4 on v3

--- a/solution.py
+++ b/solution.py
@@ -158,7 +158,7 @@
 
 ORDER = (
     "G1", "H0", "G2", "H1", "G3", "t0", "H2", "H3", "G4", "t1", "G5",
-    "F0", "T1", "F1", "F2", "T2", "F3", "S0", "t6", "S1", "S2", "t7",
+    "F0", "T1", "F1", "F2", "T2", "F3", "S0", "S1", "t6", "S2", "t7",
     "E0", "S3", "E1", "E2", "S4", "E3", "S5",
 )
 
@@ -182,9 +182,9 @@
     shard_out,
     shard_vec,
     seq_table,
-    table,
-    joined,
-    order,
+    table_hbm,
+    joined_hbm,
+    order_hbm,
     result_hbm,
     grad_hbm,
     total_in,
@@ -217,6 +217,9 @@
     work,
     stage,
     inverse_one,
+    table,
+    joined,
+    order,
     sem_a,
     sem_b,
     sem_send,
@@ -230,6 +233,7 @@
     sem_scatter_recv,
     sem_local,
     sem_slot,
+    sem_table,
 ):
     parts, per, groups = z.parts, z.per, z.groups
     me = lax.axis_index("seq")
@@ -276,6 +280,14 @@
         pl.semaphore_signal(barrier, inc=1, device_id=(me, 1 - core), device_id_type=MESH)
     greeted = parts - 1 + (1 if z.with_batch else 0)
 
+    loads = [
+        pltpu.make_async_copy(there, here, sem_table.at[n])
+        for n, (there, here) in enumerate(
+            ((table_hbm, table), (joined_hbm, joined), (order_hbm, order))
+        )
+    ]
+    for copy in loads:
+        copy.start()
     mine = shard_at((), 0)
     own_shards = [
         pltpu.make_async_copy(shard, place.at[mine], sem_local.at[w])
@@ -283,6 +295,9 @@
             ((shard_in, full.at[0]), (shard_out, full.at[1]), (shard_vec, full_vec))
         )
     ]
+    if z.with_batch:
+        rough = work.at[pl.ds(0, z.shard_rows)]
+        own_shards[1] = pltpu.make_async_copy(shard_out, rough, sem_local.at[1])
     for copy in own_shards:
         copy.start()
     send_sa[...] = jnp.zeros_like(send_sa)
@@ -332,6 +347,8 @@
 
     for copy in own_shards:
         copy.wait()
+    if z.with_batch:
+        full[1, mine] = work[0 : z.shard_rows, :].astype(BF16)
     gather_send(0)
 
     def gather_step(i):
@@ -627,6 +644,10 @@
                 sums[1, some] += into_out
                 sums[0, some] += into_in
 
+            @pl.when(g == groups - 1)
+            def _():
+                scatter_first(c)
+
             return carry
 
         lax.fori_loop(0, z.chunks, backward, 0)
@@ -659,24 +680,41 @@
 
     offsets = [sum(1 << (z.bits - 1 - i) for i in range(s)) for s in range(z.bits)]
 
+    def scatter_block(s, w, k, at, d):
+        rows = pl.ds(w * piece_rows, piece_rows)
+        full[:, at, rows] = sums[:, at, rows].astype(BF16)
+        pltpu.make_async_remote_copy(
+            src_ref=piece(at, w),
+            dst_ref=landed.at[w, offsets[s] + k],
+            send_sem=sem_scatter_send.at[w, s],
+            recv_sem=sem_scatter_recv.at[w, s],
+            device_id=partner(d),
+            device_id_type=MESH,
+        ).start()
+
+    def scatter_first(c):
+        d = z.bits - 1
+
+        def body(i, carry):
+            at = c * z.chunk_shards + 2 * i + 1 - own[d]
+            for w in range(z.pieces):
+                free = orders[w][::-1][1:]
+                k = 0
+                for n, e in enumerate(free):
+                    k = k + lax.rem(lax.div(at, weights[e]), 2) * (1 << n)
+                scatter_block(0, w, k, at, d)
+            return carry
+
+        lax.fori_loop(0, z.chunk_shards // 2, body, 0)
+
     def scatter_send(s):
         count = 1 << (z.bits - 1 - s)
-        for w in range(z.pieces):
+        for w in range(z.pieces if s > 0 else 0):
             path = orders[w][::-1]
             d, free = path[s], path[s + 1 :]
 
             def body(k, carry, w=w, d=d, free=free):
-                at = shard_at(free, k, flipped=d)
-                rows = pl.ds(w * piece_rows, piece_rows)
-                full[:, at, rows] = sums[:, at, rows].astype(BF16)
-                pltpu.make_async_remote_copy(
-                    src_ref=piece(at, w),
-                    dst_ref=landed.at[w, offsets[s] + k],
-                    send_sem=sem_scatter_send.at[w, s],
-                    recv_sem=sem_scatter_recv.at[w, s],
-                    device_id=partner(d),
-                    device_id_type=MESH,
-                ).start()
+                scatter_block(s, w, k, shard_at(free, k, flipped=d), d)
                 return carry
 
             lax.fori_loop(0, count, body, 0)
@@ -756,6 +794,8 @@
 
         return carry
 
+    for copy in loads:
+        copy.wait()
     for quarter in range(4):
         fetch(0, quarter).start()
     lax.fori_loop(0, len(steps), one_step, 0)
@@ -792,7 +832,7 @@
     shard = (2, z.shards, z.shard_rows, z.width)
     piece = (2, z.shard_rows // z.pieces, z.width)
     block = (z.glen, z.width)
-    any_space, vmem = pl.BlockSpec(memory_space=pl.ANY), pl.BlockSpec(memory_space=pltpu.VMEM)
+    any_space = pl.BlockSpec(memory_space=pl.ANY)
     dma = pltpu.SemaphoreType.DMA
     g = z.groups
     scratch = [
@@ -822,6 +862,9 @@
         pltpu.VMEM(block, F32),
         pltpu.VMEM(block, F32),
         pltpu.VMEM((z.glen, 1), F32),
+        pltpu.VMEM((z.width + 16, z.width), BF16),
+        pltpu.VMEM((z.width + 16, z.width), BF16),
+        pltpu.VMEM((z.glen, z.glen), BF16),
         dma((g,)),
         dma((g,)),
         dma((g,)),
@@ -835,6 +878,7 @@
         dma((z.pieces + 1, z.bits)),
         dma((8,)),
         dma((4,)),
+        dma((3,)),
     ]
     return pl.pallas_call(
         functools.partial(step_kernel, z),
@@ -846,7 +890,7 @@
             jax.ShapeDtypeStruct((16, z.width), F32),
             jax.ShapeDtypeStruct((z.pieces, z.shards - 1) + piece, BF16),
         ),
-        in_specs=[any_space] * 6 + [vmem] * 3,
+        in_specs=[any_space] * 9,
         out_specs=(any_space,) * 6,
         scratch_shapes=scratch,
         compiler_params=pltpu.CompilerParams(
@@ -893,7 +937,7 @@
     tokens = seqs * local
 
     shard_in = weight_in.T.astype(BF16)
-    shard_out = weight_out.astype(BF16)
+    shard_out = weight_out if z.with_batch else weight_out.astype(BF16)
     bias_shard, norm_shard = bias_ff, norm_vec
     if not z.with_batch:
         shard_in, shard_out, bias_shard = (

time: 364 us -> 361 us (level)
  no operation moved by 1% of the time
where the time goes in v4:
time: 361 us; the launch traced here: 359 us
  Pallas kernels  338 us (94%)
  local copies, waits for them, and re-layouts  10.4 us (3%)
  other arithmetic  10.1 us (3%)
    pallas_call x1, Pallas kernels, run_step(): pl.pallas_call(functools.partial(step_kernel, z), out_shape=(jax.ShapeDty...  338 us
    unnamed x6, local copies, waits for them, and re-layouts  8.81 us

profile of v4, /device:TPU:24, one launch (start us, length us, event | category | flops | bytes accessed | tf_op | source)
XLA Modules:
  0.0 359.3 jit_solution(4506431449336967534)
XLA Ops:
  0.6 1.6 convert_bitcast_fusion.shard_in
  2.3 1.3 select_maximum_fusion.shard_vec
  3.6 338.2 %shard_map.281 = (f32[2048,768]{1,0:T(8,128)}, f32[2048,768]{1,0:T(8,128)}, f32[96,768]{1,0:T(8,128)}, f32[96,768]{1,0:T(8,128)}, f32[16,768]{1,0:T(8,128)}, /*index=5*/bf16[3,31,2,32,768]{4,3,2,1,0:T(8,128)(2,1)}) custom-call(bf16[2048,768]{1,0:T(8,128)(2,1)} %bitcast.21, bf16[2048,768]{1,0:T(8,128)(2,1)} %bitcast.22, ...), custom_call_target="tpu_custom_call" | custom-call | flops 64424509440 | bytes 62914560 | tf_op jit(solution)/shard_map/pallas_call | solution.py:883
  341.8 2.2 multiply_add_fusion.2
  344.0 2.2 multiply_add_fusion
  346.2 0.0 slice-start
  346.2 0.9 slice.6
  347.1 1.3 multiply_add_fusion.5
  348.4 0.7 slice.7
  349.1 1.4 multiply_add_fusion.3
  350.5 0.0 slice-start.1
  350.5 6.1 %copy.34 = f32[8,256,768]{2,1,0:T(8,128)} copy(f32[8,256,768]{2,1,0:T(8,128)} %bitcast.19) | data formatting | bytes 12582912
  356.6 0.0 slice-done
  356.6 0.0 slice-done.1
  356.6 2.7 copy.35
  (2 shorter events, 0.0 us)
Async XLA Ops:
  346.2 10.4 %slice-start = ((s8[6291456]{0:T(1024)(128)(4,1)}), s8[2097152]{0:T(1024)(128)(4,1)S(1)}, s32[]{:S(2)}) async-start(s8[6291456]{0:T(1024)(128)(4,1)} %bitcast.16), calls=%async_computation | async-start | bytes 4194304
  350.5 6.1 %slice-start.1 = ((s8[6291456]{0:T(1024)(128)(4,1)}), s8[4194304]{0:T(1024)(128)(4,1)S(1)}, s32[]{:S(2)}) async-start(s8[6291456]{0:T(1024)(128)(4,1)} %bitcast.16), calls=%async_computation.1 | async-start | bytes 8388608
